TPU v7x, 256 devices: a whole 4x4x8 slice. The times are simulated.
256 devices in a mesh: ctx: 128 (over y, x_lo, z, core), tp: 2 (over x_hi).
Axes of the slice: x: 4 (x_hi: 2, x_lo: 2; x = x_hi * 2 + x_lo), y: 4, z: 8, core: 2. Of those that a mesh axis runs over, the one named last changes fastest.
Arguments:
- query: bfloat16 [4, 64, 128], P(None, 'tp')
- keys: bfloat16 [4, 16384, 8, 128], P(None, 'ctx', 'tp'), may hold values from -6 to 6
- values: bfloat16 [4, 16384, 8, 128], P(None, 'ctx', 'tp'), may hold values from -14 to 14
- lengths: int32 [4], replicated, may hold values from 1 to 16384, as said below
- residual: bfloat16 [4, 8192], P(None, 'ctx'), may hold values from -6 to 6
- out_weight: bfloat16 [8192, 8192], P('ctx', 'tp'), may hold values from -0.0625 to 0.0625
- norm_gain: float32 [8192], replicated, may hold values from 0.1 to 1.9
- input_weight: bfloat16 [16384, 8192], P(('ctx', 'tp')), may hold values from -0.0625 to 0.0625
- gate_weight: bfloat16 [16384, 8192], P(('ctx', 'tp')), may hold values from -0.0625 to 0.0625
- conv_weight: float32 [4, 16384], P(None, ('ctx', 'tp')), may hold values from -0.8 to 0.8
- conv_bias: float32 [16384], P(('ctx', 'tp')), may hold values from -0.5 to 0.5
- conv_state: bfloat16 [4, 3, 16384], P(None, None, ('ctx', 'tp')), may hold values from -6 to 6
- proj_weight: bfloat16 [16384, 544], P(('ctx', 'tp')), may hold values from -0.046875 to 0.046875
- step_weight: bfloat16 [16384, 512], P(('ctx', 'tp')), may hold values from -0.25 to 0.25
- step_bias: float32 [16384], P(('ctx', 'tp')), may hold values from -5 to 0.5
- decay_log: float32 [16, 16384], P(None, ('ctx', 'tp')), may hold values from -1 to 2.8
- skip_gain: float32 [16384], P(('ctx', 'tp')), may hold values from 0.5 to 1.5
- scan_state: float32 [4, 16, 16384], P(None, None, ('ctx', 'tp')), may hold values from -6 to 6
- output_weight: bfloat16 [16384, 8192], P(('ctx', 'tp')), may hold values from -0.1875 to 0.1875
Outputs:
- layer_out: bfloat16 [4, 8192], P(None, ('ctx', 'tp'))
- new_state: float32 [4, 16, 16384], P(None, None, ('ctx', 'tp'))
Inputs may be any that keep to these rules, and one draw needn't show every extreme that they name: `lengths`: some row has all 16384 positions live.
All inputs are finite; a program needn't handle non-finite values.
Results may differ from a plain program's by a relative error of at most 0.012.
Values may be sent and summed in bfloat16 or wider, within the bound.
A program may use at most 64 MiB of HBM per device.

v0:
```python
import jax
import jax.numpy as jnp
from jax import lax
from jax.sharding import PartitionSpec as P


def joined(value, axis, join):
    pieces = jax.tree.map(lambda part: lax.all_gather(part, axis), value)
    head = jax.tree.map(lambda part: part[0], pieces)
    tail = jax.tree.map(lambda part: part[1:], pieces)
    so_far, _ = lax.scan(lambda so_far, section: (join(so_far, section), None), head, tail)
    return so_far


def times_rows(left, right):
    return lax.dot_general(
        left, right, (((1,), (1,)), ((), ())), preferred_element_type=jnp.float32
    )


def merge_parts(first, second):
    highest = jnp.maximum(first[0], second[0])
    left = jnp.exp(first[0] - highest)
    right = jnp.exp(second[0] - highest)
    return (
        highest,
        first[1] * left + second[1] * right,
        first[2] * left[..., None] + second[2] * right[..., None],
    )


def on_device(
    query,
    keys,
    values,
    lengths,
    residual,
    out_weight,
    norm_gain,
    input_weight,
    gate_weight,
    conv_weight,
    conv_bias,
    conv_state,
    proj_weight,
    step_weight,
    step_bias,
    decay_log,
    skip_gain,
    scan_state,
    output_weight,
):
    decode_row_count, head_count, head_size = query.shape
    shard_len = keys.shape[1]
    kv_count = keys.shape[2]
    query_group_width = head_count // kv_count
    first_pos = lax.axis_index("ctx") * shard_len
    positions = first_pos + jnp.arange(shard_len, dtype=jnp.int32)
    live = (positions[None, :] < lengths[:, None])[:, None, None, :]
    query_rows = query.astype(jnp.float32).reshape(
        decode_row_count, kv_count, query_group_width, head_size
    )
    scores = jnp.einsum("rkgd,rtkd->rkgt", query_rows, keys.astype(jnp.float32)) * head_size ** (
        -0.5
    )
    scores = jnp.where(live, scores, -1e30)
    local_high = jnp.max(scores, axis=-1)
    weights = jnp.exp(scores - local_high[..., None]) * live.astype(jnp.float32)
    local_total = jnp.sum(weights, axis=-1)
    local_sum = jnp.einsum("rkgt,rtkd->rkgd", weights, values.astype(jnp.float32))
    highest, totals, summed = joined((local_high, local_total, local_sum), "ctx", merge_parts)
    attended = (
        (summed / totals[..., None])
        .astype(jnp.bfloat16)
        .reshape(decode_row_count, head_count * head_size)
    )
    partial_value = times_rows(attended, out_weight)
    hidden = (residual.astype(jnp.float32) + lax.psum(partial_value, "tp")).astype(jnp.bfloat16)
    whole = lax.all_gather(hidden, "ctx", axis=1, tiled=True).astype(jnp.float32)
    meansq = jnp.mean(whole * whole, axis=-1, keepdims=True)
    normed = (whole * lax.rsqrt(meansq + 1e-05) * norm_gain).astype(jnp.bfloat16)
    inputs = times_rows(normed, input_weight)
    gates = times_rows(normed, gate_weight)
    window = jnp.concatenate([conv_state.astype(jnp.float32), inputs[:, None, :]], axis=1)
    mixed_in = jax.nn.silu(jnp.sum(window * conv_weight[None], axis=1) + conv_bias)
    local_proj = jnp.dot(
        mixed_in.astype(jnp.bfloat16), proj_weight, preferred_element_type=jnp.float32
    )
    projected = lax.psum(local_proj, ("ctx", "tp"))
    rank_width = step_weight.shape[1]
    state_width = scan_state.shape[1]
    rank_part = projected[:, :rank_width].astype(jnp.bfloat16)
    entry_map = projected[:, rank_width : rank_width + state_width]
    exit_map = projected[:, rank_width + state_width :]
    step = jax.nn.softplus(times_rows(rank_part, step_weight) + step_bias)
    decay = jnp.exp(-step[:, None, :] * jnp.exp(decay_log)[None])
    new_state = decay * scan_state + step[:, None, :] * entry_map[:, :, None] * mixed_in[:, None, :]
    gated = (
        (jnp.sum(new_state * exit_map[:, :, None], axis=1) + skip_gain * mixed_in)
        * jax.nn.silu(gates)
    ).astype(jnp.bfloat16)
    term = jnp.dot(gated, output_weight, preferred_element_type=jnp.float32)
    mixed_out = lax.psum_scatter(term, ("ctx", "tp"), scatter_dimension=1, tiled=True)
    out_width = mixed_out.shape[1]
    own_part = lax.dynamic_slice_in_dim(hidden, lax.axis_index("tp") * out_width, out_width, 1)
    layer_out = (own_part.astype(jnp.float32) + mixed_out).astype(jnp.bfloat16)
    return (layer_out, new_state)


def solution(mesh):
    placed = (
        P(None, "tp", None),
        P(None, "ctx", "tp", None),
        P(None, "ctx", "tp", None),
        P(),
        P(None, "ctx"),
        P("ctx", "tp"),
        P(),
        P(("ctx", "tp"), None),
        P(("ctx", "tp"), None),
        P(None, ("ctx", "tp")),
        P(("ctx", "tp")),
        P(None, None, ("ctx", "tp")),
        P(("ctx", "tp"), None),
        P(("ctx", "tp"), None),
        P(("ctx", "tp")),
        P(None, ("ctx", "tp")),
        P(("ctx", "tp")),
        P(None, None, ("ctx", "tp")),
        P(("ctx", "tp"), None),
    )
    return jax.shard_map(
        on_device,
        mesh=mesh,
        in_specs=placed,
        out_specs=(P(None, ("ctx", "tp")), P(None, None, ("ctx", "tp"))),
        check_vma=False,
    )
```

profile of v0, /device:TPU:1, one launch (start us, length us, event | category | flops | bytes accessed | tf_op | source)
XLA Modules:
  0.0 1985.0 jit_solution(14164698501406246331)
XLA Ops:
  8.0 1.5 fusion.28
  9.6 2.0 fusion.4
  11.6 164.8 %all-gather = f32[512,4,8]{2,1,0:T(4,128)S(1)} all-gather(f32[4,4,8]{2,1,0:T(4,128)S(1)} %get-tuple-element.66), channel_id=2, replica_groups=mesh['ctx'=128,'tp'=2] {'ctx'}, dimensions={0}, use_global_device_ids=true | all-gather | bytes 66048 | tf_op jit(solution)/shard_map/all_gather | solution.py:8
  176.7 153.9 %all-gather.1 = f32[512,4,8]{2,1,0:T(4,128)S(1)} all-gather(f32[4,4,8]{2,1,0:T(4,128)S(1)} %fusion.7), channel_id=3, replica_groups=mesh['ctx'=128,'tp'=2] {'ctx'}, dimensions={0}, use_global_device_ids=true | all-gather | bytes 66048 | tf_op jit(solution)/shard_map/all_gather | solution.py:8
  332.2 7.6 slice.48
  339.9 128.0 %while.14 = (s32[]{:T(128)}, f32[4,4,8]{2,1,0:T(4,128)S(1)}, f32[4,4,8]{2,1,0:T(4,128)S(1)}, f32[4,4,8,128]{3,2,1,0:T(8,128)S(1)}, f32[127,4,4,8]{3,2,1,0:T(4,12...) while((s32[]{:T(128)}, f32[4,4,8]{2,1,0:T(4,128)S(1)}, ...), condition=%wide.region_3.4_spmd, body=%wide.region_2.3_spmd.sunk | while | flops 49922 | bytes 201829 | solution.py:11
  340.9 1.0 fusion.39
  341.9 1.0 fusion.39
  342.9 1.0 fusion.39
  343.9 1.0 fusion.39
  344.9 1.0 fusion.39
  345.9 1.0 fusion.39
  346.9 1.0 fusion.39
  347.9 1.0 fusion.39
  349.0 1.0 fusion.39
  350.0 1.0 fusion.39
  351.0 1.0 fusion.39
  352.0 1.0 fusion.39
  353.0 1.0 fusion.39
  354.0 1.0 fusion.39
  355.0 1.0 fusion.39
  356.0 1.0 fusion.39
  357.0 1.0 fusion.39
  358.0 1.0 fusion.39
  359.0 1.0 fusion.39
  360.0 1.0 fusion.39
  361.1 1.0 fusion.39
  362.1 1.0 fusion.39
  363.1 1.0 fusion.39
  364.1 1.0 fusion.39
  365.1 1.0 fusion.39
  366.1 1.0 fusion.39
  367.1 1.0 fusion.39
  368.1 1.0 fusion.39
  369.1 1.0 fusion.39
  370.1 1.0 fusion.39
  371.1 1.0 fusion.39
  372.1 1.0 fusion.39
  373.2 1.0 fusion.39
  374.2 1.0 fusion.39
  375.2 1.0 fusion.39
  376.2 1.0 fusion.39
  382.2 1.0 fusion.39
  383.2 1.0 fusion.39
  384.2 1.0 fusion.39
  401.4 1.0 fusion.39
  402.4 1.0 fusion.39
  403.4 1.0 fusion.39
  420.6 1.0 fusion.39
  421.6 1.0 fusion.39
  422.6 1.0 fusion.39
  439.7 1.0 fusion.39
  440.7 1.0 fusion.39
  441.7 1.0 fusion.39
  458.9 1.0 fusion.39
  459.9 1.0 fusion.39
  460.9 1.0 fusion.39
  468.0 1.3 fusion.8
  469.3 5.3 psum.14
  474.6 153.9 %all-gather.3 = bf16[128,64,4]{1,2,0:T(4,128)(2,1)S(1)} all-gather(bf16[1,64,4]{1,2,0:T(4,128)(2,1)S(1)} %bitcast.53), channel_id=1, replica_groups=mesh['ctx'=128,'tp'=2] {'ctx'}, dimensions={0}, use_global_device_ids=true | all-gather | bytes 66048 | tf_op jit(solution)/shard_map/all_gather | solution.py:79
  629.0 1.6 convolution_bitcast_fusion.1
  630.9 73.2 %psum.15 = f32[4,544]{1,0:T(4,128)S(1)} all-reduce(f32[4,544]{1,0:T(4,128)S(1)} %fusion.20), channel_id=1, replica_groups=mesh['ctx'=128,'tp'=2] {'ctx','tp'}, use_global_device_ids=true, to_apply=%region_7.8 | all-reduce | flops 2176 | bytes 17408 | tf_op jit(solution)/shard_map/psum | solution.py:89
  705.0 4.8 convolution_bitcast_fusion
  709.9 1266.9 %reduce-scatter.4.cloned.1.call-done = f32[32,4]{1,0:T(8,128)} async-done(((f32[8192,4]{1,0:T(8,128)}), f32[32,4]{1,0:T(8,128)}) %reduce-scatter.4.cloned.1.call-update) | async-done | bytes 528
  (254 shorter events, 82.3 us)
Async XLA Ops:
  7.2 697.9 %copy-start = (bf16[64,8192]{1,0:T(8,128)(2,1)S(1)}, bf16[64,8192]{1,0:T(8,128)(2,1)}, u32[]{:S(2)}) copy-start(bf16[64,8192]{1,0:T(8,128)(2,1)} %param.39) | copy-start | bytes 3145732
  7.2 324.9 %all-gather.6.cloned.1.call-start = ((), (), s32[]{:S(2)}) async-start(), calls=%async_computation.1 | async-start | bytes 8454144 | tf_op jit(solution)/shard_map/all_gather | solution.py:8
  11.6 1965.2 %reduce-scatter.4.cloned.1.call-start = ((), (), s32[]{:S(2)}) async-start(), calls=%async_computation.2 | async-start | bytes 4210688
  332.1 7.7 slice-start
  332.1 142.5 %copy-start.6 = (bf16[4,64]{1,0:T(4,128)(2,1)S(1)}, bf16[4,64]{1,0:T(4,128)(2,1)}, u32[]{:S(2)}) copy-start(bf16[4,64]{1,0:T(4,128)(2,1)} %param.25) | copy-start | bytes 1540
  332.1 296.9 %copy-start.1 = (f32[8192]{0:T(1024)S(1)}, f32[8192]{0:T(1024)}, u32[]{:S(2)}) copy-start(f32[8192]{0:T(1024)} %param.27) | copy-start | bytes 98308
  332.1 298.6 %copy-start.5 = (f32[4,64]{1,0:T(4,128)S(1)}, f32[4,64]{1,0:T(4,128)}, u32[]{:S(2)}) copy-start(f32[4,64]{1,0:T(4,128)} %param.30) | copy-start | bytes 3076
  332.1 298.6 %copy-start.9 = (f32[64]{0:T(128)S(1)}, f32[64]{0:T(128)}, u32[]{:S(2)}) copy-start(f32[64]{0:T(128)} %param.31) | copy-start | bytes 772
  332.2 298.6 %copy-start.2 = (bf16[64,544]{1,0:T(8,128)(2,1)S(1)}, bf16[64,544]{1,0:T(8,128)(2,1)}, u32[]{:S(2)}) copy-start(bf16[64,544]{1,0:T(8,128)(2,1)} %param.33) | copy-start | bytes 208900
  332.2 372.0 %copy-start.3 = (bf16[64,512]{1,0:T(8,128)(2,1)S(1)}, bf16[64,512]{1,0:T(8,128)(2,1)}, u32[]{:S(2)}) copy-start(bf16[64,512]{1,0:T(8,128)(2,1)} %param.34) | copy-start | bytes 196612
  332.2 372.0 %copy-start.7 = (f32[64]{0:T(128)S(1)}, f32[64]{0:T(128)}, u32[]{:S(2)}) copy-start(f32[64]{0:T(128)} %param.35) | copy-start | bytes 772
  332.2 372.1 %copy-start.4 = (f32[4,16,64]{2,1,0:T(8,128)S(1)}, f32[4,16,64]{2,1,0:T(8,128)}, u32[]{:S(2)}) copy-start(f32[4,16,64]{2,1,0:T(8,128)} %param.38) | copy-start | bytes 49156
  332.2 372.8 %copy-start.8 = (f32[64]{0:T(128)S(1)}, f32[64]{0:T(128)}, u32[]{:S(2)}) copy-start(f32[64]{0:T(128)} %param.37) | copy-start | bytes 772
Sparse Core Ops, SparseCore 0:
  11.7 223.9 all-gather.5
  710.0 1266.6 reduce-scatter.3
where the time goes:
time: 1990 us
  waiting for transfers between devices  1270 us (64%)
  blocking collectives  551 us (28%)
  other arithmetic  128 us (6%)
    unnamed x3, waiting for transfers between devices  1270 us
    all_gather x2, blocking collectives, joined(): pieces = jax.tree.map(lambda part: lax.all_gather(part, axis), value)  319 us
    all_gather x1, blocking collectives, on_device(): lax.all_gather(hidden, 'ctx', axis=1, tiled=True).astype(jnp.float32)  154 us
    add x127, other arithmetic, merge_parts(): first[2] * left[..., None] + second[2] * right[..., None]  121 us
    psum x1, blocking collectives, on_device(): projected = lax.psum(local_proj, ('ctx', 'tp'))  73.2 us
  transfers between devices with their start and end apart: 2, of which 1 were waited for; matrix products, arithmetic and copies ran while one was open for 0% of the time, Pallas kernels for 0%

commit v1 on v0

v1 whole, which is shorter than its diff:
```python
import functools

import jax
import jax.numpy as jnp
from jax import lax
from jax.experimental import pallas as pl
from jax.experimental.pallas import tpu as pltpu
from jax.sharding import PartitionSpec as P

MESH = pl.DeviceIdType.MESH
F32 = jnp.float32
BF16 = jnp.bfloat16


def far_first(n):
    return sorted(range(1, n), key=lambda d: -min(d, n - d))


def nt(left, right):
    return lax.dot_general(
        left, right, (((1,), (1,)), ((), ())), preferred_element_type=F32
    )


def silu(x):
    return x * (1.0 / (1.0 + jnp.exp(-x)))


def softplus(x):
    return jnp.maximum(x, 0.0) + jnp.log1p(jnp.exp(-jnp.abs(x)))


def iota(shape, dim):
    return lax.broadcasted_iota(jnp.int32, shape, dim)


def kernel(*refs):
    names_in = (
        "q", "k", "v", "res", "ow", "gain", "iw", "gw", "cw", "cb", "cs", "pw",
        "sw", "sb", "dl", "sg", "ss", "outw",
    )
    n_in = len(names_in)
    lengths = refs[0]
    hbm = dict(zip(names_in, refs[1 : 1 + n_in]))
    lo_ref, ns_ref = refs[1 + n_in : 3 + n_in]
    vm = dict(zip(names_in, refs[3 + n_in : 3 + 2 * n_in]))
    (
        obuf, r_o, ob, mlb, att, attf, hb, w2, p_a, r_pa, p_b, r_pb,
        tb, r_t, tz, r_z, tc, r_c, nsb, in_sem, send_sem, recv_sem, out_sem,
    ) = refs[3 + 2 * n_in :]

    c = lax.axis_index("ctx")
    h = lax.axis_index("tp")
    a = lax.div(c, 16)
    b = lax.rem(c, 16)
    z = lax.div(b, 2)
    core = lax.rem(b, 2)
    e = a * 2 + h

    def in_a8(d):
        other = lax.rem(a + d, 8)
        return other, (other * 16 + b, h)

    def in_a16(d):
        other = lax.rem(e + d, 16)
        return other, (lax.div(other, 2) * 16 + b, lax.rem(other, 2))

    def in_b16(d):
        other = lax.rem(b + d, 16)
        return other, (a * 16 + other, h)

    def in_z(d):
        other = lax.rem(z + d, 8)
        return other, (a * 16 + other * 2 + core, h)

    corners = (
        (a * 16 + b, 1 - h),
        (a * 16 + z * 2 + (1 - core), h),
        (a * 16 + z * 2 + (1 - core), 1 - h),
    )

    loads = {
        name: pltpu.make_async_copy(hbm[name], vm[name], in_sem.at[i])
        for i, name in enumerate(names_in)
    }
    for name in names_in:
        loads[name].start()

    barrier = pltpu.get_barrier_semaphore()
    greeted = [in_a16(d)[1] for d in far_first(16)]
    greeted += [in_b16(d)[1] for d in far_first(16)] + [corners[2]]
    for peer in greeted:
        pl.semaphore_signal(barrier, 1, device_id=peer, device_id_type=MESH)

    def send(src, dst, stage, peer):
        pltpu.make_async_remote_copy(
            src, dst, send_sem.at[stage], recv_sem.at[stage],
            device_id=peer, device_id_type=MESH,
        ).start()

    def arrived(block, stage):
        pltpu.make_async_copy(block, block, recv_sem.at[stage]).wait()

    def sent(block, stage):
        pltpu.make_async_copy(block, block, send_sem.at[stage]).wait()

    for name in ("q", "k", "v"):
        loads[name].wait()
    shape = (32, 512)
    column = iota(shape, 1)
    same_head = lax.rem(column, 4) == lax.div(iota(shape, 0), 8)
    position = c * 128 + lax.div(column, 4)
    lane16 = iota((16, 128), 1)
    for r in range(4):
        scores = nt(vm["q"][r], vm["k"][r]) * (128.0 ** -0.5)
        live = jnp.logical_and(same_head, position < lengths[r])
        scores = jnp.where(live, scores, -1e30)
        high = jnp.max(scores, axis=1, keepdims=True)
        weights = jnp.where(live, jnp.exp(scores - high), 0.0)
        total = jnp.sum(weights, axis=1, keepdims=True)
        summed = jnp.dot(
            weights.astype(BF16), vm["v"][r], preferred_element_type=F32
        )
        for half in range(2):
            rows = slice(half * 16, half * 16 + 16)
            obuf[2 * r + half, 0] = summed[rows]
            obuf[2 * r + half, 1] = jnp.where(lane16 < 64, high[rows], total[rows])

    pl.semaphore_wait(barrier, len(greeted))

    for d in far_first(8):
        other, peer = in_a8(d)
        send(obuf.at[other], r_o.at[d - 1], 0, peer)
    arrived(r_o, 0)
    parts = [(obuf[a, 0], obuf[a, 1])] + [(r_o[i, 0], r_o[i, 1]) for i in range(7)]
    highs = [ml[:, 0:1] for _, ml in parts]
    totals = [ml[:, 64:65] for _, ml in parts]
    top = functools.reduce(jnp.maximum, highs)
    scales = [jnp.exp(high - top) for high in highs]
    total = sum(s * t for s, t in zip(scales, totals))
    summed = sum(s * o for s, (o, _) in zip(scales, parts))

    on_diag = lane16 == iota((16, 128), 0)
    ob[b] = summed.astype(BF16)
    mlb[b, 0:1] = jnp.sum(jnp.where(on_diag, top, 0.0), axis=0, keepdims=True)
    mlb[b, 1:2] = jnp.sum(jnp.where(on_diag, total, 0.0), axis=0, keepdims=True)
    for d in far_first(16):
        _, peer = in_b16(d)
        send(mlb.at[b], mlb.at[b], 1, peer)
        send(ob.at[b], ob.at[b], 2, peer)
    arrived(mlb.at[pl.ds(0, 15)], 1)
    high_rows = mlb[:, 0, :]
    total_rows = mlb[:, 1, :]
    scale_rows = jnp.exp(high_rows - jnp.max(high_rows, axis=0, keepdims=True))
    all_total = jnp.sum(scale_rows * total_rows, axis=0, keepdims=True)
    valid = iota((1, 128), 1) < 16
    scale_rows = scale_rows / jnp.where(valid, all_total, 1.0)
    columns = [
        jnp.sum(jnp.where(on_diag, scale_rows[i : i + 1], 0.0), axis=1, keepdims=True)
        for i in range(16)
    ]
    arrived(ob.at[pl.ds(0, 15)], 2)
    attended = sum(columns[i] * ob[i].astype(F32) for i in range(16))

    att[a] = attended.astype(BF16)
    for d in far_first(8):
        _, peer = in_a8(d)
        send(att.at[a], att.at[a], 3, peer)
    loads["ow"].wait()
    loads["res"].wait()
    arrived(att.at[pl.ds(0, 7)], 3)
    for i in range(8):
        attf[i // 2, (i % 2) * 16 : (i % 2) * 16 + 16] = att[i].astype(F32)
    flat = jnp.concatenate([attf[:, i, :] for i in range(32)], axis=1).astype(BF16)
    partial = nt(flat, vm["ow"][...])
    partial = partial + jnp.where(h == 0, vm["res"][...].astype(F32), 0.0)

    twice = jnp.concatenate([partial, partial], axis=1)
    hb[b] = jnp.where(lax.div(iota((4, 128), 1), 64) == core, twice, 0.0)
    for d in far_first(16):
        _, peer = in_b16(d)
        send(hb.at[b], hb.at[b], 4, peer)
    arrived(hb.at[pl.ds(0, 15)], 4)
    halves = hb[...].reshape(8, 2, 4, 128)
    w2[e] = halves[:, 0] + halves[:, 1]
    for d in far_first(16):
        _, peer = in_a16(d)
        send(w2.at[e], w2.at[e], 5, peer)
    for name in ("gain", "iw", "gw", "cw", "cb", "cs", "pw"):
        loads[name].wait()
    conv = vm["cb"][...]
    for i in range(3):
        conv = conv + vm["cs"][i].astype(F32) * vm["cw"][i : i + 1]
    arrived(w2.at[pl.ds(0, 15)], 5)
    pairs = w2[...].reshape(8, 2, 8, 4, 128)
    hidden = (pairs[:, 0] + pairs[:, 1]).astype(BF16).astype(F32)
    square = jnp.sum(jnp.sum(hidden * hidden, axis=(0, 1)), axis=1, keepdims=True)
    scale = lax.rsqrt(square * (1.0 / 8192.0) + 1e-5)
    gain = vm["gain"][...]
    normed = jnp.concatenate(
        [
            hidden[i // 8, i % 8] * scale * gain[i : i + 1]
            for i in range(64)
        ],
        axis=1,
    ).astype(BF16)
    inputs = nt(normed, vm["iw"][...])
    mixed = silu(conv + inputs * vm["cw"][3:4])

    local = jnp.dot(mixed.astype(BF16), vm["pw"][...], preferred_element_type=F32)
    for i in range(4):
        p_a[i] = local[:, i * 128 : i * 128 + 128]
    p_a[4] = jnp.concatenate([local[:, 512:544], jnp.zeros((4, 96), F32)], axis=1)
    for d in far_first(16):
        _, peer = in_a16(d)
        send(p_a, r_pa.at[d - 1], 6, peer)
    gates = silu(nt(normed, vm["gw"][...]))
    for name in ("sw", "sb", "dl", "sg", "ss", "outw"):
        loads[name].wait()
    rate = jnp.exp(vm["dl"][...])
    arrived(r_pa, 6)
    p_b[...] = p_a[...] + jnp.sum(r_pa[...], axis=0)
    for d in far_first(16):
        _, peer = in_b16(d)
        send(p_b, r_pb.at[d - 1], 7, peer)
    arrived(r_pb, 7)
    projected = p_b[...] + jnp.sum(r_pb[...], axis=0)

    rank = jnp.concatenate([projected[i] for i in range(4)], axis=1).astype(BF16)
    step = softplus(nt(rank, vm["sw"][...]) + vm["sb"][...])
    maps = projected[4]
    pick_exit = lane16 == iota((16, 128), 0) + 16
    skip = vm["sg"][...] * mixed
    rows = []
    for r in range(4):
        entry = jnp.sum(jnp.where(on_diag, maps[r : r + 1], 0.0), axis=1, keepdims=True)
        leave = jnp.sum(jnp.where(pick_exit, maps[r : r + 1], 0.0), axis=1, keepdims=True)
        step_r = step[r : r + 1]
        state = jnp.exp(-step_r * rate) * vm["ss"][r] + entry * (step_r * mixed[r : r + 1])
        nsb[r] = state
        rows.append(jnp.sum(state * leave, axis=0, keepdims=True))
    store = pltpu.make_async_copy(nsb, ns_ref, out_sem)
    store.start()
    gated = ((jnp.concatenate(rows, axis=0) + skip) * gates).astype(BF16)

    term = jnp.dot(gated, vm["outw"][...], preferred_element_type=F32)
    for i in range(64):
        tb[i // 8, i % 8] = term[:, i * 128 : i * 128 + 128]
    for d in far_first(8):
        other, peer = in_a8(d)
        send(tb.at[other], r_t.at[d - 1], 8, peer)
    arrived(r_t, 8)
    tz[...] = tb[a] + jnp.sum(r_t[...], axis=0)
    for d in far_first(8):
        other, peer = in_z(d)
        send(tz.at[other], r_z.at[d - 1], 9, peer)
    arrived(r_z, 9)
    tc[...] = tz[z] + jnp.sum(r_z[...], axis=0)
    for i, peer in enumerate(corners):
        send(tc, r_c.at[i], 10, peer)
    own = (w2[2 * a, z] + w2[2 * a + 1, z]).astype(BF16).astype(F32)
    arrived(r_c, 10)
    whole = tc[...] + jnp.sum(r_c[...], axis=0) + own
    place = core * 2 + h
    picked = whole[:, 0:32]
    for i in range(1, 4):
        picked = jnp.where(place == i, whole[:, i * 32 : i * 32 + 32], picked)
    lo_ref[...] = picked

    store.wait()
    sent(r_o, 0)
    sent(mlb.at[pl.ds(0, 15)], 1)
    sent(ob.at[pl.ds(0, 15)], 2)
    sent(att.at[pl.ds(0, 7)], 3)
    sent(hb.at[pl.ds(0, 15)], 4)
    sent(w2.at[pl.ds(0, 15)], 5)
    sent(r_pa, 6)
    sent(r_pb, 7)
    sent(r_t, 8)
    sent(r_z, 9)
    sent(r_c, 10)


def on_device(
    query, keys, values, lengths, residual, out_weight, norm_gain, input_weight,
    gate_weight, conv_weight, conv_bias, conv_state, proj_weight, step_weight,
    step_bias, decay_log, skip_gain, scan_state, output_weight,
):
    operands = (
        query,
        keys.reshape(4, 512, 128),
        values.reshape(4, 512, 128),
        residual,
        out_weight,
        norm_gain.reshape(64, 128),
        input_weight,
        gate_weight,
        conv_weight,
        conv_bias.reshape(1, 64),
        conv_state.transpose(1, 0, 2),
        proj_weight,
        step_weight,
        step_bias.reshape(1, 64),
        decay_log,
        skip_gain.reshape(1, 64),
        scan_state,
        output_weight,
    )
    vmem = [pltpu.VMEM(x.shape, x.dtype) for x in operands]
    scratch = [
        pltpu.VMEM((8, 2, 16, 128), F32),
        pltpu.VMEM((7, 2, 16, 128), F32),
        pltpu.VMEM((16, 16, 128), BF16),
        pltpu.VMEM((16, 2, 128), F32),
        pltpu.VMEM((8, 16, 128), BF16),
        pltpu.VMEM((4, 32, 128), F32),
        pltpu.VMEM((16, 4, 128), F32),
        pltpu.VMEM((16, 8, 4, 128), F32),
        pltpu.VMEM((5, 4, 128), F32),
        pltpu.VMEM((15, 5, 4, 128), F32),
        pltpu.VMEM((5, 4, 128), F32),
        pltpu.VMEM((15, 5, 4, 128), F32),
        pltpu.VMEM((8, 8, 4, 128), F32),
        pltpu.VMEM((7, 8, 4, 128), F32),
        pltpu.VMEM((8, 4, 128), F32),
        pltpu.VMEM((7, 4, 128), F32),
        pltpu.VMEM((4, 128), F32),
        pltpu.VMEM((3, 4, 128), F32),
        pltpu.VMEM((4, 16, 64), F32),
        pltpu.SemaphoreType.DMA((len(operands),)),
        pltpu.SemaphoreType.DMA((11,)),
        pltpu.SemaphoreType.DMA((11,)),
        pltpu.SemaphoreType.DMA,
    ]
    layer_out, new_state = pl.pallas_call(
        kernel,
        out_shape=(
            jax.ShapeDtypeStruct((4, 32), F32),
            jax.ShapeDtypeStruct((4, 16, 64), F32),
        ),
        in_specs=[pl.BlockSpec(memory_space=pltpu.SMEM)]
        + [pl.BlockSpec(memory_space=pltpu.HBM)] * len(operands),
        out_specs=(
            pl.BlockSpec(memory_space=pltpu.VMEM),
            pl.BlockSpec(memory_space=pltpu.HBM),
        ),
        scratch_shapes=vmem + scratch,
        compiler_params=pltpu.CompilerParams(
            collective_id=0, has_side_effects=True, vmem_limit_bytes=56 << 20
        ),
        name="decode_step",
    )(lengths, *operands)
    return layer_out.astype(BF16), new_state


def solution(mesh):
    placed = (
        P(None, "tp", None),
        P(None, "ctx", "tp", None),
        P(None, "ctx", "tp", None),
        P(),
        P(None, "ctx"),
        P("ctx", "tp"),
        P(),
        P(("ctx", "tp"), None),
        P(("ctx", "tp"), None),
        P(None, ("ctx", "tp")),
        P(("ctx", "tp")),
        P(None, None, ("ctx", "tp")),
        P(("ctx", "tp"), None),
        P(("ctx", "tp"), None),
        P(("ctx", "tp")),
        P(None, ("ctx", "tp")),
        P(("ctx", "tp")),
        P(None, None, ("ctx", "tp")),
        P(("ctx", "tp"), None),
    )
    return jax.shard_map(
        on_device,
        mesh=mesh,
        in_specs=placed,
        out_specs=(P(None, ("ctx", "tp")), P(None, None, ("ctx", "tp"))),
        check_vma=False,
    )
```

time: 1990 us -> 64.7 us (0.03)
  waiting for transfers between devices: 1270 us -> 0 us
  blocking collectives: 551 us -> 0 us
  other arithmetic: 128 us -> 0.56 us
  Pallas kernels: 0 us -> 61.3 us
    unnamed x3 -> x0, waiting for transfers between devices: 1270 us -> none
    all_gather x3 -> x0, blocking collectives: 473 us -> none  [the longest x2 319 us: joined(): pieces = jax.tree.map(lambda part: lax.all_gather(part, axis), value)]
    add x255 -> x0, other arithmetic: 125 us -> none  [the longest x127 121 us: merge_parts(): first[2] * left[..., None] + second[2] * right[..., None]]
    psum x2 -> x0, blocking collectives: 78.5 us -> none  [the longest x1 73.2 us: on_device(): projected = lax.psum(local_proj, ('ctx', 'tp'))]
    pallas_call x0 -> x1, Pallas kernels: none -> 61.3 us  [on_device(): pl.pallas_call(kernel, out_shape=(jax.ShapeDtypeStruct((4, 32), F32), jax...]
  transfers between devices with their start and end apart: 2 -> 0, of which waited for: 1 -> 0; matrix products, arithmetic and copies ran while one was open for 0% -> 0% of each run, Pallas kernels for 0% -> 0%
where the time goes in v1:
time: 64.7 us; the launch traced here: 64.5 us
  Pallas kernels  61.3 us (95%)
  local copies, waits for them, and re-layouts  2.02 us (3%)
  between operations  0.66 us (1%)
    pallas_call x1, Pallas kernels, on_device(): pl.pallas_call(kernel, out_shape=(jax.ShapeDtypeStruct((4, 32), F32), jax...  61.3 us
    unnamed x3, local copies, waits for them, and re-layouts  2.02 us

profile of v1, /device:TPU:1, one launch (start us, length us, event | category | flops | bytes accessed | tf_op | source)
XLA Modules:
  0.0 64.5 jit_solution(17921627167101020927)
XLA Ops:
  0.6 61.3 %decode_step.1 = (f32[4,32]{1,0:T(4,128)}, f32[4,16,64]{2,1,0:T(8,128)}) custom-call(s32[4]{0:T(128)} %refs_0_.1, bf16[4,32,128]{2,1,0:T(8,128)(2,1)} %refs_1_.1, bf16[4,512,128]{2,1,0:T(8,128)(2,1)} %bitcast.7, bf16[4,512,128]{2,1,0:T(8,128)(2,1)} %bitcast.8, bf16[4,64]{1,0:T(4,128)(2,1)} %refs_4_.1, bf16[64,4096]{1,0:T(8,128)(2,1)} %refs_5_.1, ...), custom_call_target="tpu_custom_call" | custom-call | tf_op jit(solution)/shard_map/decode_step/pallas_call | solution.py:335
  61.9 0.0 copy-start
  61.9 0.6 %copy-done = f32[4,32]{1,0:T(4,128)S(1)} copy-done((f32[4,32]{1,0:T(4,128)S(1)}, f32[4,32]{1,0:T(4,128)}, u32[]{:S(2)}) %copy-start) | copy-done | bytes 536
  62.6 0.6 convert_element_type.3
  63.1 1.4 %copy.22 = f32[4,16,64]{2,1,0:T(8,128)} copy(f32[4,16,64]{2,1,0:T(8,128)} %get-tuple-element.9) | data formatting | bytes 32768
Async XLA Ops:
  61.9 0.7 %copy-start = (f32[4,32]{1,0:T(4,128)S(1)}, f32[4,32]{1,0:T(4,128)}, u32[]{:S(2)}) copy-start(f32[4,32]{1,0:T(4,128)} %get-tuple-element.4) | copy-start | bytes 1540

commit v2 on v1

v2 whole, which is shorter than its diff:
```python
import functools

import jax
import jax.numpy as jnp
from jax import lax
from jax.experimental import pallas as pl
from jax.experimental.pallas import tpu as pltpu
from jax.sharding import PartitionSpec as P

MESH = pl.DeviceIdType.MESH
F32 = jnp.float32
BF16 = jnp.bfloat16


def far_first(n):
    return sorted(range(1, n), key=lambda d: -min(d, n - d))


def nt(left, right):
    return lax.dot_general(
        left, right, (((1,), (1,)), ((), ())), preferred_element_type=F32
    )


def silu(x):
    return x * (1.0 / (1.0 + jnp.exp(-x)))


def softplus(x):
    return jnp.maximum(x, 0.0) + jnp.log1p(jnp.exp(-jnp.abs(x)))


def iota(shape, dim):
    return lax.broadcasted_iota(jnp.int32, shape, dim)


def kernel(*refs):
    names_in = (
        "len", "q", "k", "v", "res", "ow", "gain", "iw", "gw", "cw", "cb", "cs",
        "pw", "sw", "sb", "dl", "sg", "ss", "outw",
    )
    n_in = len(names_in)
    hbm = dict(zip(names_in, refs[:n_in]))
    lo_ref, ns_ref = refs[n_in : 2 + n_in]
    vm = dict(zip(names_in, refs[2 + n_in : 2 + 2 * n_in]))
    (
        obuf, r_o, mid, r_m, att, hb, w2, p_a, r_pa, rank_b, r_rank, maps_b,
        r_maps, tb, r_t, tz, r_z, in_sem, send_sem, recv_sem,
    ) = refs[2 + 2 * n_in :]

    c = lax.axis_index("ctx")
    h = lax.axis_index("tp")
    a = lax.div(c, 16)
    b = lax.rem(c, 16)
    z = lax.div(b, 2)
    core = lax.rem(b, 2)
    e = a * 2 + h
    g = a * 2 + core

    def in_yx(d):
        other = lax.rem(e + d, 16)
        return other, (lax.div(other, 2) * 16 + b, lax.rem(other, 2))

    def in_b16(d):
        other = lax.rem(b + d, 16)
        return other, (a * 16 + other, h)

    def in_g16(d):
        other = lax.rem(g + d, 16)
        return other, (lax.div(other, 2) * 16 + z * 2 + lax.rem(other, 2), h)

    def in_z(d):
        other = lax.rem(z + d, 8)
        return other, (a * 16 + other * 2 + core, h)

    loads = {
        name: pltpu.make_async_copy(hbm[name], vm[name], in_sem.at[i])
        for i, name in enumerate(names_in)
    }

    def need(*names):
        for name in names:
            loads.pop(name).wait()

    first = ("k", "q", "len", "v")
    for name in first:
        loads[name].start()

    barrier = pltpu.get_barrier_semaphore()
    greeted = [in_b16(d)[1] for d in far_first(16)]
    greeted += [in_yx(d)[1] for d in far_first(16)]
    greeted += [
        (lax.rem(a + d, 8) * 16 + z * 2 + (1 - core), h) for d in far_first(8)
    ]
    for peer in greeted:
        pl.semaphore_signal(barrier, 1, device_id=peer, device_id_type=MESH)

    def send(src, dst, stage, peer):
        pltpu.make_async_remote_copy(
            src, dst, send_sem.at[stage], recv_sem.at[stage],
            device_id=peer, device_id_type=MESH,
        ).start()

    def arrived(block, stage):
        pltpu.make_async_copy(block, block, recv_sem.at[stage]).wait()

    pending = []

    def sent(block, stage):
        pltpu.make_async_copy(block, block, send_sem.at[stage]).wait()

    shape = (32, 512)
    column = iota(shape, 1)
    same_head = lax.rem(column, 4) == lax.div(iota(shape, 0), 8)
    position = c * 128 + lax.div(column, 4)
    lane8 = iota((8, 128), 1)
    need(*first)
    for r in range(4):
        scores = nt(vm["q"][r], vm["k"][r]) * (128.0 ** -0.5)
        live = jnp.logical_and(same_head, position < vm["len"][r])
        scores = jnp.where(live, scores, -1e30)
        high = jnp.max(scores, axis=1, keepdims=True)
        weights = jnp.where(live, jnp.exp(scores - high), 0.0)
        total = jnp.sum(weights, axis=1, keepdims=True)
        summed = jnp.dot(
            weights.astype(BF16), vm["v"][r], preferred_element_type=F32
        )
        for i in range(4):
            rows = slice(i * 8, i * 8 + 8)
            obuf[4 * r + i, 0] = summed[rows]
            obuf[4 * r + i, 1] = jnp.where(lane8 < 64, high[rows], total[rows])

    pl.semaphore_wait(barrier, len(greeted))

    for d in far_first(16):
        other, peer = in_g16(d)
        send(obuf.at[other], r_o.at[d - 1], 0, peer)
    pending.append((r_o, 0))
    for name in names_in:
        if name not in first:
            loads[name].start()

    def merge(parts):
        highs = [ml[:, 0:1] for _, ml in parts]
        totals = [ml[:, 64:65] for _, ml in parts]
        top = functools.reduce(jnp.maximum, highs)
        scales = [jnp.exp(high - top) for high in highs]
        total = sum(s * t for s, t in zip(scales, totals))
        return top, total, sum(s * o for s, (o, _) in zip(scales, parts))

    arrived(r_o, 0)
    top, total, summed = merge(
        [(obuf[g, 0], obuf[g, 1])] + [(r_o[i, 0], r_o[i, 1]) for i in range(15)]
    )
    mid[0] = summed
    mid[1] = jnp.where(lane8 < 64, top, total)

    for d in far_first(8):
        _, peer = in_z(d)
        send(mid, r_m.at[d - 1], 1, peer)
    pending.append((r_m, 1))
    arrived(r_m, 1)
    _, total, summed = merge(
        [(mid[0], mid[1])] + [(r_m[i, 0], r_m[i, 1]) for i in range(7)]
    )

    att[g] = summed / total
    for d in far_first(16):
        _, peer = in_g16(d)
        send(att.at[g], att.at[g], 2, peer)
    pending.append((att.at[pl.ds(0, 15)], 2))
    need("ow", "res")
    arrived(att.at[pl.ds(0, 15)], 2)
    heads = att[...].reshape(4, 4, 8, 128)
    flat = jnp.concatenate(
        [heads[:, i // 8, i % 8, :] for i in range(32)], axis=1
    ).astype(BF16)
    partial = nt(flat, vm["ow"][...])
    partial = partial + jnp.where(h == 0, vm["res"][...].astype(F32), 0.0)

    twice = jnp.concatenate([partial, partial], axis=1)
    hb[b] = jnp.where(lax.div(iota((4, 128), 1), 64) == core, twice, 0.0)
    for d in far_first(16):
        _, peer = in_b16(d)
        send(hb.at[b], hb.at[b], 4, peer)
    pending.append((hb.at[pl.ds(0, 15)], 4))
    arrived(hb.at[pl.ds(0, 15)], 4)
    halves = hb[...].reshape(8, 2, 4, 128)
    w2[e] = (halves[:, 0] + halves[:, 1]).reshape(32, 128).astype(BF16)
    for d in far_first(16):
        _, peer = in_yx(d)
        send(w2.at[e], w2.at[e], 5, peer)
    pending.append((w2.at[pl.ds(0, 15)], 5))
    need("gain", "iw", "gw", "cw", "cb", "cs", "pw")
    conv = vm["cb"][...]
    for i in range(3):
        conv = conv + vm["cs"][i].astype(F32) * vm["cw"][i : i + 1]
    arrived(w2.at[pl.ds(0, 15)], 5)

    def whole_hidden(block):
        both = w2[2 * block].astype(F32) + w2[2 * block + 1].astype(F32)
        return both.astype(BF16).astype(F32)

    hidden = [whole_hidden(i) for i in range(8)]
    squares = jnp.sum(sum(x * x for x in hidden), axis=1, keepdims=True)
    square = sum(squares[i * 4 : i * 4 + 4] for i in range(8))
    scale = lax.rsqrt(square * (1.0 / 8192.0) + 1e-5)
    gain = vm["gain"][...]
    normed = jnp.concatenate(
        [
            hidden[i // 8][i % 8 * 4 : i % 8 * 4 + 4] * scale * gain[i : i + 1]
            for i in range(64)
        ],
        axis=1,
    ).astype(BF16)
    inputs = nt(normed, vm["iw"][...])
    mixed = silu(conv + inputs * vm["cw"][3:4])

    local = jnp.dot(mixed.astype(BF16), vm["pw"][...], preferred_element_type=F32)
    for i in range(4):
        p_a[i] = local[:, i * 128 : i * 128 + 128]
    p_a[4] = jnp.concatenate([local[:, 512:544], jnp.zeros((4, 96), F32)], axis=1)
    for d in far_first(16):
        _, peer = in_yx(d)
        send(p_a, r_pa.at[d - 1], 6, peer)
    pending.append((r_pa, 6))
    gates = silu(nt(normed, vm["gw"][...]))
    need("sw", "sb", "dl", "sg", "ss", "outw")
    rate = jnp.exp(vm["dl"][...])
    skip = vm["sg"][...] * mixed
    arrived(r_pa, 6)
    projected = p_a[...] + jnp.sum(r_pa[...], axis=0)
    ranks = projected[0:4].reshape(16, 128)
    rank_b[...] = ranks.astype(BF16)
    maps_b[...] = projected[4]
    for d in far_first(16):
        _, peer = in_b16(d)
        send(rank_b, r_rank.at[d - 1], 7, peer)
        send(maps_b, r_maps.at[d - 1], 8, peer)
    pending.append((r_rank, 7))
    pending.append((r_maps, 8))
    arrived(r_rank, 7)
    ranks = ranks + jnp.sum(r_rank[...].astype(F32), axis=0)
    arrived(r_maps, 8)
    maps = maps_b[...] + jnp.sum(r_maps[...], axis=0)

    rank = jnp.concatenate(
        [ranks[i * 4 : i * 4 + 4] for i in range(4)], axis=1
    ).astype(BF16)
    step = softplus(nt(rank, vm["sw"][...]) + vm["sb"][...])
    lane16 = iota((16, 128), 1)
    pick_entry = lane16 == iota((16, 128), 0)
    pick_leave = lane16 == iota((16, 128), 0) + 16
    rows = []
    for r in range(4):
        row = maps[r : r + 1]
        entry = jnp.sum(jnp.where(pick_entry, row, 0.0), axis=1, keepdims=True)
        leave = jnp.sum(jnp.where(pick_leave, row, 0.0), axis=1, keepdims=True)
        step_r = step[r : r + 1]
        state = jnp.exp(-step_r * rate) * vm["ss"][r] + entry * (step_r * mixed[r : r + 1])
        ns_ref[r] = state
        rows.append(jnp.sum(state * leave, axis=0, keepdims=True))
    gated = ((jnp.concatenate(rows, axis=0) + skip) * gates).astype(BF16)

    term = jnp.dot(gated, vm["outw"][...], preferred_element_type=F32)
    for i in range(8):
        tb[i] = jnp.concatenate(
            [
                term[:, (i * 8 + k) * 128 : (i * 8 + k) * 128 + 128]
                for k in range(8)
            ],
            axis=0,
        ).astype(BF16)
    for d in far_first(16):
        other, peer = in_yx(d)
        send(tb.at[lax.div(other, 2)], r_t.at[d - 1], 9, peer)
    pending.append((r_t, 9))
    mine = whole_hidden(a)
    own = sum(
        jnp.where(z == i, mine[i * 4 : i * 4 + 4], 0.0) for i in range(8)
    )
    arrived(r_t, 9)
    summed = tb[a].astype(F32) + jnp.sum(r_t[...].astype(F32), axis=0)
    tz[...] = summed.reshape(8, 4, 128)
    for d in far_first(16):
        other, peer = in_b16(d)
        send(tz.at[lax.div(other, 2)], r_z.at[d - 1], 10, peer)
    pending.append((r_z, 10))
    arrived(r_z, 10)
    whole = tz[z] + jnp.sum(r_z[...], axis=0) + own
    place = core * 2 + h
    picked = whole[:, 0:32]
    for i in range(1, 4):
        picked = jnp.where(place == i, whole[:, i * 32 : i * 32 + 32], picked)
    lo_ref[...] = picked

    for block, stage in pending:
        sent(block, stage)


def on_device(
    query, keys, values, lengths, residual, out_weight, norm_gain, input_weight,
    gate_weight, conv_weight, conv_bias, conv_state, proj_weight, step_weight,
    step_bias, decay_log, skip_gain, scan_state, output_weight,
):
    operands = (
        lengths,
        query,
        keys.reshape(4, 512, 128),
        values.reshape(4, 512, 128),
        residual,
        out_weight,
        norm_gain.reshape(64, 128),
        input_weight,
        gate_weight,
        conv_weight,
        conv_bias.reshape(1, 64),
        conv_state.transpose(1, 0, 2),
        proj_weight,
        step_weight,
        step_bias.reshape(1, 64),
        decay_log,
        skip_gain.reshape(1, 64),
        scan_state,
        output_weight,
    )
    operands = [
        pltpu.with_memory_space_constraint(x, pltpu.HBM) for x in operands
    ]
    held = [pltpu.SMEM(lengths.shape, lengths.dtype)]
    held += [pltpu.VMEM(x.shape, x.dtype) for x in operands[1:]]
    scratch = [
        pltpu.VMEM((16, 2, 8, 128), F32),
        pltpu.VMEM((15, 2, 8, 128), F32),
        pltpu.VMEM((2, 8, 128), F32),
        pltpu.VMEM((7, 2, 8, 128), F32),
        pltpu.VMEM((16, 8, 128), F32),
        pltpu.VMEM((16, 4, 128), F32),
        pltpu.VMEM((16, 32, 128), BF16),
        pltpu.VMEM((5, 4, 128), F32),
        pltpu.VMEM((15, 5, 4, 128), F32),
        pltpu.VMEM((16, 128), BF16),
        pltpu.VMEM((15, 16, 128), BF16),
        pltpu.VMEM((4, 128), F32),
        pltpu.VMEM((15, 4, 128), F32),
        pltpu.VMEM((8, 32, 128), BF16),
        pltpu.VMEM((15, 32, 128), BF16),
        pltpu.VMEM((8, 4, 128), F32),
        pltpu.VMEM((15, 4, 128), F32),
        pltpu.SemaphoreType.DMA((len(operands),)),
        pltpu.SemaphoreType.DMA((11,)),
        pltpu.SemaphoreType.DMA((11,)),
    ]
    layer_out, new_state = pl.pallas_call(
        kernel,
        out_shape=(
            jax.ShapeDtypeStruct((4, 32), F32),
            jax.ShapeDtypeStruct((4, 16, 64), F32),
        ),
        in_specs=[pl.BlockSpec(memory_space=pltpu.HBM)] * len(operands),
        out_specs=(
            pl.BlockSpec(memory_space=pltpu.VMEM),
            pl.BlockSpec(memory_space=pltpu.VMEM),
        ),
        scratch_shapes=held + scratch,
        compiler_params=pltpu.CompilerParams(
            collective_id=0, has_side_effects=True, vmem_limit_bytes=24 << 20
        ),
        name="decode_step",
    )(*operands)
    return layer_out.astype(BF16), new_state


def solution(mesh):
    placed = (
        P(None, "tp", None),
        P(None, "ctx", "tp", None),
        P(None, "ctx", "tp", None),
        P(),
        P(None, "ctx"),
        P("ctx", "tp"),
        P(),
        P(("ctx", "tp"), None),
        P(("ctx", "tp"), None),
        P(None, ("ctx", "tp")),
        P(("ctx", "tp")),
        P(None, None, ("ctx", "tp")),
        P(("ctx", "tp"), None),
        P(("ctx", "tp"), None),
        P(("ctx", "tp")),
        P(None, ("ctx", "tp")),
        P(("ctx", "tp")),
        P(None, None, ("ctx", "tp")),
        P(("ctx", "tp"), None),
    )
    return jax.shard_map(
        on_device,
        mesh=mesh,
        in_specs=placed,
        out_specs=(P(None, ("ctx", "tp")), P(None, None, ("ctx", "tp"))),
        check_vma=False,
    )
```

time: 64.7 us -> 57.6 us (0.89)
  Pallas kernels: 61.3 us -> 55.7 us
  local copies, waits for them, and re-layouts: 2.02 us -> 0.61 us
    pallas_call x1, Pallas kernels: 61.3 us -> 55.7 us  [on_device(): pl.pallas_call(kernel, out_shape=(jax.ShapeDtypeStruct((4, 32), F32), jax...]
    unnamed x3 -> x1, local copies, waits for them, and re-layouts: 2.02 us -> 0.61 us
where the time goes in v2:
time: 57.6 us; the launch traced here: 57.5 us
  Pallas kernels  55.7 us (97%)
  between operations  0.65 us (1%)
  local copies, waits for them, and re-layouts  0.61 us (1%)
    pallas_call x1, Pallas kernels, on_device(): pl.pallas_call(kernel, out_shape=(jax.ShapeDtypeStruct((4, 32), F32), jax...  55.7 us

profile of v2, /device:TPU:1, one launch (start us, length us, event | category | flops | bytes accessed | tf_op | source)
XLA Modules:
  0.0 57.5 jit_solution(7699706424420970108)
XLA Ops:
  0.6 55.7 %decode_step.1 = (f32[4,32]{1,0:T(4,128)S(1)}, f32[4,16,64]{2,1,0:T(8,128)S(1)}) custom-call(s32[4]{0:T(128)} %refs_0_.1, bf16[4,32,128]{2,1,0:T(8,128)(2,1)} %refs_1_.1, bf16[4,512,128]{2,1,0:T(8,128)(2,1)} %bitcast.7, bf16[4,512,128]{2,1,0:T(8,128)(2,1)} %bitcast.8, bf16[4,64]{1,0:T(4,128)(2,1)} %refs_4_.1, bf16[64,4096]{1,0:T(8,128)(2,1)} %refs_5_.1, ...), custom_call_target="tpu_custom_call" | custom-call | tf_op jit(solution)/shard_map/decode_step/pallas_call | solution.py:354
  56.3 0.6 convert_element_type.3
  56.9 0.6 %copy.22 = f32[4,16,64]{2,1,0:T(8,128)} copy(f32[4,16,64]{2,1,0:T(8,128)S(1)} %get-tuple-element.9) | data formatting | bytes 32768

commit v3 on v2

--- a/solution.py
+++ b/solution.py
@@ -36,17 +36,18 @@
 
 def kernel(*refs):
     names_in = (
-        "len", "q", "k", "v", "res", "ow", "gain", "iw", "gw", "cw", "cb", "cs",
-        "pw", "sw", "sb", "dl", "sg", "ss", "outw",
+        "len", "q", "k", "v", "res", "gain", "iw", "gw", "cw", "cb", "cs", "pw",
+        "sw", "sb", "dl", "sg", "ss", "outw",
     )
     n_in = len(names_in)
+    ow = refs[n_in]
     hbm = dict(zip(names_in, refs[:n_in]))
-    lo_ref, ns_ref = refs[n_in : 2 + n_in]
-    vm = dict(zip(names_in, refs[2 + n_in : 2 + 2 * n_in]))
+    lo_ref, ns_ref = refs[n_in + 1 : n_in + 3]
+    vm = dict(zip(names_in, refs[n_in + 3 : 2 * n_in + 3]))
     (
-        obuf, r_o, mid, r_m, att, hb, w2, p_a, r_pa, rank_b, r_rank, maps_b,
-        r_maps, tb, r_t, tz, r_z, in_sem, send_sem, recv_sem,
-    ) = refs[2 + 2 * n_in :]
+        obuf, r_o, ob, mlb, attf, wo, hp, r_hp, h2, p_a, r_pa, rank_b, r_rank,
+        maps_b, r_maps, tb, r_t, tz, r_z, in_sem, own_sem, send_sem, recv_sem,
+    ) = refs[2 * n_in + 3 :]
 
     c = lax.axis_index("ctx")
     h = lax.axis_index("tp")
@@ -55,7 +56,10 @@
     z = lax.div(b, 2)
     core = lax.rem(b, 2)
     e = a * 2 + h
-    g = a * 2 + core
+
+    def in_a8(d):
+        other = lax.rem(a + d, 8)
+        return other, (other * 16 + b, h)
 
     def in_yx(d):
         other = lax.rem(e + d, 16)
@@ -64,14 +68,6 @@
     def in_b16(d):
         other = lax.rem(b + d, 16)
         return other, (a * 16 + other, h)
-
-    def in_g16(d):
-        other = lax.rem(g + d, 16)
-        return other, (lax.div(other, 2) * 16 + z * 2 + lax.rem(other, 2), h)
-
-    def in_z(d):
-        other = lax.rem(z + d, 8)
-        return other, (a * 16 + other * 2 + core, h)
 
     loads = {
         name: pltpu.make_async_copy(hbm[name], vm[name], in_sem.at[i])
@@ -88,10 +84,7 @@
 
     barrier = pltpu.get_barrier_semaphore()
     greeted = [in_b16(d)[1] for d in far_first(16)]
-    greeted += [in_yx(d)[1] for d in far_first(16)]
-    greeted += [
-        (lax.rem(a + d, 8) * 16 + z * 2 + (1 - core), h) for d in far_first(8)
-    ]
+    greeted += [in_a8(d)[1] for d in far_first(8)] + [(c, 1 - h)]
     for peer in greeted:
         pl.semaphore_signal(barrier, 1, device_id=peer, device_id_type=MESH)
 
@@ -113,7 +106,9 @@
     column = iota(shape, 1)
     same_head = lax.rem(column, 4) == lax.div(iota(shape, 0), 8)
     position = c * 128 + lax.div(column, 4)
-    lane8 = iota((8, 128), 1)
+    lane16 = iota((16, 128), 1)
+    on_diag = lane16 == iota((16, 128), 0)
+    low4 = iota((4, 128), 1) < 64
     need(*first)
     for r in range(4):
         scores = nt(vm["q"][r], vm["k"][r]) * (128.0 ** -0.5)
@@ -125,94 +120,116 @@
         summed = jnp.dot(
             weights.astype(BF16), vm["v"][r], preferred_element_type=F32
         )
-        for i in range(4):
-            rows = slice(i * 8, i * 8 + 8)
-            obuf[4 * r + i, 0] = summed[rows]
-            obuf[4 * r + i, 1] = jnp.where(lane8 < 64, high[rows], total[rows])
+        for i in range(8):
+            rows = slice(i * 4, i * 4 + 4)
+            obuf[i, 0, r * 4 : r * 4 + 4] = summed[rows]
+            obuf[i, 1, r * 4 : r * 4 + 4] = jnp.where(low4, high[rows], total[rows])
 
     pl.semaphore_wait(barrier, len(greeted))
 
-    for d in far_first(16):
-        other, peer = in_g16(d)
+    for d in far_first(8):
+        other, peer = in_a8(d)
         send(obuf.at[other], r_o.at[d - 1], 0, peer)
     pending.append((r_o, 0))
+
+    def columns_of(device):
+        return ow.at[:, pl.ds(pl.multiple_of(device * 512, 512), 512)]
+
+    mine = wo.at[pl.ds(pl.multiple_of(a * 64, 64), 64)]
+    for d in far_first(8):
+        other, peer = in_a8(d)
+        send(columns_of(other), mine, 1, peer)
+    pending.append((wo.at[pl.ds(0, 448)], 1))
+    own_columns = pltpu.make_async_copy(columns_of(a), mine, own_sem)
+    own_columns.start()
     for name in names_in:
         if name not in first:
             loads[name].start()
 
-    def merge(parts):
-        highs = [ml[:, 0:1] for _, ml in parts]
-        totals = [ml[:, 64:65] for _, ml in parts]
-        top = functools.reduce(jnp.maximum, highs)
-        scales = [jnp.exp(high - top) for high in highs]
-        total = sum(s * t for s, t in zip(scales, totals))
-        return top, total, sum(s * o for s, (o, _) in zip(scales, parts))
-
     arrived(r_o, 0)
-    top, total, summed = merge(
-        [(obuf[g, 0], obuf[g, 1])] + [(r_o[i, 0], r_o[i, 1]) for i in range(15)]
-    )
-    mid[0] = summed
-    mid[1] = jnp.where(lane8 < 64, top, total)
-
-    for d in far_first(8):
-        _, peer = in_z(d)
-        send(mid, r_m.at[d - 1], 1, peer)
-    pending.append((r_m, 1))
-    arrived(r_m, 1)
-    _, total, summed = merge(
-        [(mid[0], mid[1])] + [(r_m[i, 0], r_m[i, 1]) for i in range(7)]
-    )
-
-    att[g] = summed / total
-    for d in far_first(16):
-        _, peer = in_g16(d)
-        send(att.at[g], att.at[g], 2, peer)
-    pending.append((att.at[pl.ds(0, 15)], 2))
-    need("ow", "res")
-    arrived(att.at[pl.ds(0, 15)], 2)
-    heads = att[...].reshape(4, 4, 8, 128)
-    flat = jnp.concatenate(
-        [heads[:, i // 8, i % 8, :] for i in range(32)], axis=1
-    ).astype(BF16)
-    partial = nt(flat, vm["ow"][...])
-    partial = partial + jnp.where(h == 0, vm["res"][...].astype(F32), 0.0)
-
-    twice = jnp.concatenate([partial, partial], axis=1)
-    hb[b] = jnp.where(lax.div(iota((4, 128), 1), 64) == core, twice, 0.0)
+    parts = [(obuf[a, 0], obuf[a, 1])] + [(r_o[i, 0], r_o[i, 1]) for i in range(7)]
+    highs = [ml[:, 0:1] for _, ml in parts]
+    totals = [ml[:, 64:65] for _, ml in parts]
+    top = functools.reduce(jnp.maximum, highs)
+    scales = [jnp.exp(high - top) for high in highs]
+    total = sum(s * t for s, t in zip(scales, totals))
+    summed = sum(s * o for s, (o, _) in zip(scales, parts))
+
+    ob[b] = summed.astype(BF16)
+    mlb[b, 0:1] = jnp.sum(jnp.where(on_diag, top, 0.0), axis=0, keepdims=True)
+    mlb[b, 1:2] = jnp.sum(jnp.where(on_diag, total, 0.0), axis=0, keepdims=True)
     for d in far_first(16):
         _, peer = in_b16(d)
-        send(hb.at[b], hb.at[b], 4, peer)
-    pending.append((hb.at[pl.ds(0, 15)], 4))
-    arrived(hb.at[pl.ds(0, 15)], 4)
-    halves = hb[...].reshape(8, 2, 4, 128)
-    w2[e] = (halves[:, 0] + halves[:, 1]).reshape(32, 128).astype(BF16)
+        send(mlb.at[b], mlb.at[b], 2, peer)
+        send(ob.at[b], ob.at[b], 3, peer)
+    pending.append((mlb.at[pl.ds(0, 15)], 2))
+    pending.append((ob.at[pl.ds(0, 15)], 3))
+    arrived(mlb.at[pl.ds(0, 15)], 2)
+    high_rows = mlb[:, 0, :]
+    total_rows = mlb[:, 1, :]
+    scale_rows = jnp.exp(high_rows - jnp.max(high_rows, axis=0, keepdims=True))
+    all_total = jnp.sum(scale_rows * total_rows, axis=0, keepdims=True)
+    valid = iota((1, 128), 1) < 16
+    scale_rows = scale_rows / jnp.where(valid, all_total, 1.0)
+    columns = [
+        jnp.sum(jnp.where(on_diag, scale_rows[i : i + 1], 0.0), axis=1, keepdims=True)
+        for i in range(16)
+    ]
+    arrived(ob.at[pl.ds(0, 15)], 3)
+    attended = sum(columns[i] * ob[i].astype(F32) for i in range(16))
+
+    for r in range(4):
+        attf[r] = attended[r * 4 : r * 4 + 4]
+    flat = jnp.concatenate([attf[:, i, :] for i in range(4)], axis=1).astype(BF16)
+    need("res")
+    own_columns.wait()
+    arrived(wo.at[pl.ds(0, 448)], 1)
+    partial = nt(flat, wo[...])
+    rest = vm["res"][...].astype(F32)
+    twice = jnp.concatenate([rest, rest], axis=1)
+    adds = jnp.logical_and(low4 == (lax.rem(a, 2) == 0), h == 0)
+    rest = jnp.where(adds, twice, 0.0)
+    for i in range(4):
+        hp[i] = partial[:, i * 128 : i * 128 + 128] + jnp.where(
+            lax.div(a, 2) == i, rest, 0.0
+        )
+
     for d in far_first(16):
         _, peer = in_yx(d)
-        send(w2.at[e], w2.at[e], 5, peer)
-    pending.append((w2.at[pl.ds(0, 15)], 5))
+        send(hp, r_hp.at[d - 1], 4, peer)
+    pending.append((r_hp, 4))
+    arrived(r_hp, 4)
+    h2[b] = (hp[...] + jnp.sum(r_hp[...], axis=0)).reshape(16, 128).astype(BF16)
+    for d in far_first(16):
+        _, peer = in_b16(d)
+        send(h2.at[b], h2.at[b], 5, peer)
+    pending.append((h2.at[pl.ds(0, 15)], 5))
     need("gain", "iw", "gw", "cw", "cb", "cs", "pw")
     conv = vm["cb"][...]
     for i in range(3):
         conv = conv + vm["cs"][i].astype(F32) * vm["cw"][i : i + 1]
-    arrived(w2.at[pl.ds(0, 15)], 5)
-
-    def whole_hidden(block):
-        both = w2[2 * block].astype(F32) + w2[2 * block + 1].astype(F32)
-        return both.astype(BF16).astype(F32)
-
-    hidden = [whole_hidden(i) for i in range(8)]
-    squares = jnp.sum(sum(x * x for x in hidden), axis=1, keepdims=True)
-    square = sum(squares[i * 4 : i * 4 + 4] for i in range(8))
+    arrived(h2.at[pl.ds(0, 15)], 5)
+
+    def swapped(x):
+        return jnp.concatenate([x[:, 64:], x[:, :64]], axis=1)
+
+    low16 = lane16 < 64
+    evens, odds = [], []
+    for i in range(8):
+        left = h2[2 * i].astype(F32)
+        right = h2[2 * i + 1].astype(F32)
+        evens.append(jnp.where(low16, left, swapped(right)))
+        odds.append(jnp.where(low16, swapped(left), right))
+    squares = jnp.sum(sum(x * x for x in evens + odds), axis=1, keepdims=True)
+    square = sum(squares[i * 4 : i * 4 + 4] for i in range(4))
     scale = lax.rsqrt(square * (1.0 / 8192.0) + 1e-5)
     gain = vm["gain"][...]
-    normed = jnp.concatenate(
-        [
-            hidden[i // 8][i % 8 * 4 : i % 8 * 4 + 4] * scale * gain[i : i + 1]
-            for i in range(64)
-        ],
-        axis=1,
-    ).astype(BF16)
+    blocks = []
+    for i in range(64):
+        block = (odds if i // 8 % 2 else evens)[i % 8]
+        row = i // 16 * 4
+        blocks.append(block[row : row + 4] * scale * gain[i : i + 1])
+    normed = jnp.concatenate(blocks, axis=1).astype(BF16)
     inputs = nt(normed, vm["iw"][...])
     mixed = silu(conv + inputs * vm["cw"][3:4])
 
@@ -248,13 +265,11 @@
         [ranks[i * 4 : i * 4 + 4] for i in range(4)], axis=1
     ).astype(BF16)
     step = softplus(nt(rank, vm["sw"][...]) + vm["sb"][...])
-    lane16 = iota((16, 128), 1)
-    pick_entry = lane16 == iota((16, 128), 0)
     pick_leave = lane16 == iota((16, 128), 0) + 16
     rows = []
     for r in range(4):
         row = maps[r : r + 1]
-        entry = jnp.sum(jnp.where(pick_entry, row, 0.0), axis=1, keepdims=True)
+        entry = jnp.sum(jnp.where(on_diag, row, 0.0), axis=1, keepdims=True)
         leave = jnp.sum(jnp.where(pick_leave, row, 0.0), axis=1, keepdims=True)
         step_r = step[r : r + 1]
         state = jnp.exp(-step_r * rate) * vm["ss"][r] + entry * (step_r * mixed[r : r + 1])
@@ -275,10 +290,18 @@
         other, peer = in_yx(d)
         send(tb.at[lax.div(other, 2)], r_t.at[d - 1], 9, peer)
     pending.append((r_t, 9))
-    mine = whole_hidden(a)
-    own = sum(
-        jnp.where(z == i, mine[i * 4 : i * 4 + 4], 0.0) for i in range(8)
-    )
+    near = h2[b].astype(F32)
+    near = sum(
+        jnp.where(lax.div(a, 2) == i, near[i * 4 : i * 4 + 4], 0.0) for i in range(4)
+    )
+
+    def quarter(block, place):
+        picked = block[:, 0:32]
+        for i in range(1, 4):
+            picked = jnp.where(place == i, block[:, i * 32 : i * 32 + 32], picked)
+        return picked
+
+    own = quarter(near, lax.rem(a, 2) * 2 + h)
     arrived(r_t, 9)
     summed = tb[a].astype(F32) + jnp.sum(r_t[...].astype(F32), axis=0)
     tz[...] = summed.reshape(8, 4, 128)
@@ -287,12 +310,8 @@
         send(tz.at[lax.div(other, 2)], r_z.at[d - 1], 10, peer)
     pending.append((r_z, 10))
     arrived(r_z, 10)
-    whole = tz[z] + jnp.sum(r_z[...], axis=0) + own
-    place = core * 2 + h
-    picked = whole[:, 0:32]
-    for i in range(1, 4):
-        picked = jnp.where(place == i, whole[:, i * 32 : i * 32 + 32], picked)
-    lo_ref[...] = picked
+    whole = tz[z] + jnp.sum(r_z[...], axis=0)
+    lo_ref[...] = quarter(whole, core * 2 + h) + own
 
     for block, stage in pending:
         sent(block, stage)
@@ -309,7 +328,6 @@
         keys.reshape(4, 512, 128),
         values.reshape(4, 512, 128),
         residual,
-        out_weight,
         norm_gain.reshape(64, 128),
         input_weight,
         gate_weight,
@@ -324,19 +342,22 @@
         scan_state,
         output_weight,
     )
-    operands = [
-        pltpu.with_memory_space_constraint(x, pltpu.HBM) for x in operands
-    ]
     held = [pltpu.SMEM(lengths.shape, lengths.dtype)]
     held += [pltpu.VMEM(x.shape, x.dtype) for x in operands[1:]]
+    operands = [
+        pltpu.with_memory_space_constraint(x, pltpu.HBM)
+        for x in operands + (out_weight,)
+    ]
     scratch = [
-        pltpu.VMEM((16, 2, 8, 128), F32),
-        pltpu.VMEM((15, 2, 8, 128), F32),
-        pltpu.VMEM((2, 8, 128), F32),
-        pltpu.VMEM((7, 2, 8, 128), F32),
-        pltpu.VMEM((16, 8, 128), F32),
-        pltpu.VMEM((16, 4, 128), F32),
-        pltpu.VMEM((16, 32, 128), BF16),
+        pltpu.VMEM((8, 2, 16, 128), F32),
+        pltpu.VMEM((7, 2, 16, 128), F32),
+        pltpu.VMEM((16, 16, 128), BF16),
+        pltpu.VMEM((16, 2, 128), F32),
+        pltpu.VMEM((4, 4, 128), F32),
+        pltpu.VMEM((512, 512), BF16),
+        pltpu.VMEM((4, 4, 128), F32),
+        pltpu.VMEM((15, 4, 4, 128), F32),
+        pltpu.VMEM((16, 16, 128), BF16),
         pltpu.VMEM((5, 4, 128), F32),
         pltpu.VMEM((15, 5, 4, 128), F32),
         pltpu.VMEM((16, 128), BF16),
@@ -347,7 +368,8 @@
         pltpu.VMEM((15, 32, 128), BF16),
         pltpu.VMEM((8, 4, 128), F32),
         pltpu.VMEM((15, 4, 128), F32),
-        pltpu.SemaphoreType.DMA((len(operands),)),
+        pltpu.SemaphoreType.DMA((len(held),)),
+        pltpu.SemaphoreType.DMA,
         pltpu.SemaphoreType.DMA((11,)),
         pltpu.SemaphoreType.DMA((11,)),
     ]

time: 57.6 us -> 56 us (0.972)
  Pallas kernels: 55.7 us -> 54.1 us
    pallas_call x1, Pallas kernels: 55.7 us -> 54.1 us  [on_device(): pl.pallas_call(kernel, out_shape=(jax.ShapeDtypeStruct((4, 32), F32), jax...]
where the time goes in v3:
time: 56 us; the launch traced here: 55.9 us
  Pallas kernels  54.1 us (97%)
  between operations  0.65 us (1%)
  local copies, waits for them, and re-layouts  0.61 us (1%)
  other arithmetic  0.56 us (1%)
    pallas_call x1, Pallas kernels, on_device(): pl.pallas_call(kernel, out_shape=(jax.ShapeDtypeStruct((4, 32), F32), jax...  54.1 us

profile of v3, /device:TPU:1, one launch (start us, length us, event | category | flops | bytes accessed | tf_op | source)
XLA Modules:
  0.0 55.9 jit_solution(5574219109420533238)
XLA Ops:
  0.6 54.1 %decode_step.1 = (f32[4,32]{1,0:T(4,128)S(1)}, f32[4,16,64]{2,1,0:T(8,128)S(1)}) custom-call(s32[4]{0:T(128)} %refs_0_.1, bf16[4,32,128]{2,1,0:T(8,128)(2,1)} %refs_1_.1, bf16[4,512,128]{2,1,0:T(8,128)(2,1)} %bitcast.7, bf16[4,512,128]{2,1,0:T(8,128)(2,1)} %bitcast.8, bf16[4,64]{1,0:T(4,128)(2,1)} %refs_4_.1, f32[64,128]{1,0:T(8,128)} %bitcast.9, ...), custom_call_target="tpu_custom_call" | custom-call | tf_op jit(solution)/shard_map/decode_step/pallas_call | solution.py:376
  54.7 0.6 %convert_element_type.3 = bf16[4,32]{1,0:T(4,128)(2,1)} convert(f32[4,32]{1,0:T(4,128)S(1)} %get-tuple-element.4) | non-fusion elementwise | flops 128 | bytes 768 | tf_op jit(solution)/shard_map/convert_element_type | solution.py:393
  55.3 0.6 %copy.22 = f32[4,16,64]{2,1,0:T(8,128)} copy(f32[4,16,64]{2,1,0:T(8,128)S(1)} %get-tuple-element.9) | data formatting | bytes 32768

commit v4 on v3

--- a/solution.py
+++ b/solution.py
@@ -46,7 +46,7 @@
     vm = dict(zip(names_in, refs[n_in + 3 : 2 * n_in + 3]))
     (
         obuf, r_o, ob, mlb, attf, wo, hp, r_hp, h2, p_a, r_pa, rank_b, r_rank,
-        maps_b, r_maps, tb, r_t, tz, r_z, in_sem, own_sem, send_sem, recv_sem,
+        maps_b, r_maps, tb, r_t, tz, r_z, in_sem, own_sem, chip_sem, send_sem, recv_sem,
     ) = refs[2 * n_in + 3 :]
 
     c = lax.axis_index("ctx")
@@ -130,7 +130,7 @@
     for d in far_first(8):
         other, peer = in_a8(d)
         send(obuf.at[other], r_o.at[d - 1], 0, peer)
-    pending.append((r_o, 0))
+    sent(r_o, 0)
 
     def columns_of(device):
         return ow.at[:, pl.ds(pl.multiple_of(device * 512, 512), 512)]
@@ -147,17 +147,23 @@
             loads[name].start()
 
     arrived(r_o, 0)
-    parts = [(obuf[a, 0], obuf[a, 1])] + [(r_o[i, 0], r_o[i, 1]) for i in range(7)]
-    highs = [ml[:, 0:1] for _, ml in parts]
-    totals = [ml[:, 64:65] for _, ml in parts]
+    low16 = lane16 < 64
+
+    def swapped(x):
+        return jnp.concatenate([x[:, 64:], x[:, :64]], axis=1)
+
+    outs = [obuf[a, 0]] + [r_o[i, 0] for i in range(7)]
+    marks = [obuf[a, 1]] + [r_o[i, 1] for i in range(7)]
+    highs = [jnp.where(low16, x, swapped(x)) for x in marks]
     top = functools.reduce(jnp.maximum, highs)
-    scales = [jnp.exp(high - top) for high in highs]
-    total = sum(s * t for s, t in zip(scales, totals))
-    summed = sum(s * o for s, (o, _) in zip(scales, parts))
+    scales = [jnp.exp(x - top) for x in highs]
+    total = sum(s * x for s, x in zip(scales, marks))
+    summed = sum(s * x for s, x in zip(scales, outs))
 
     ob[b] = summed.astype(BF16)
-    mlb[b, 0:1] = jnp.sum(jnp.where(on_diag, top, 0.0), axis=0, keepdims=True)
-    mlb[b, 1:2] = jnp.sum(jnp.where(on_diag, total, 0.0), axis=0, keepdims=True)
+    packed = jnp.where(low16, top, total)
+    both = jnp.logical_or(on_diag, lane16 == iota((16, 128), 0) + 64)
+    mlb[b] = jnp.sum(jnp.where(both, packed, 0.0), axis=0, keepdims=True)
     for d in far_first(16):
         _, peer = in_b16(d)
         send(mlb.at[b], mlb.at[b], 2, peer)
@@ -166,7 +172,7 @@
     pending.append((ob.at[pl.ds(0, 15)], 3))
     arrived(mlb.at[pl.ds(0, 15)], 2)
     high_rows = mlb[:, 0, :]
-    total_rows = mlb[:, 1, :]
+    total_rows = swapped(high_rows)
     scale_rows = jnp.exp(high_rows - jnp.max(high_rows, axis=0, keepdims=True))
     all_total = jnp.sum(scale_rows * total_rows, axis=0, keepdims=True)
     valid = iota((1, 128), 1) < 16
@@ -202,35 +208,51 @@
     h2[b] = (hp[...] + jnp.sum(r_hp[...], axis=0)).reshape(16, 128).astype(BF16)
     for d in far_first(16):
         _, peer = in_b16(d)
-        send(h2.at[b], h2.at[b], 5, peer)
+        pltpu.make_async_remote_copy(
+            h2.at[b], h2.at[b], send_sem.at[5], chip_sem.at[b],
+            device_id=peer, device_id_type=MESH,
+        ).start()
     pending.append((h2.at[pl.ds(0, 15)], 5))
     need("gain", "iw", "gw", "cw", "cb", "cs", "pw")
     conv = vm["cb"][...]
     for i in range(3):
         conv = conv + vm["cs"][i].astype(F32) * vm["cw"][i : i + 1]
-    arrived(h2.at[pl.ds(0, 15)], 5)
-
-    def swapped(x):
-        return jnp.concatenate([x[:, 64:], x[:, :64]], axis=1)
-
-    low16 = lane16 < 64
-    evens, odds = [], []
-    for i in range(8):
-        left = h2[2 * i].astype(F32)
-        right = h2[2 * i + 1].astype(F32)
-        evens.append(jnp.where(low16, left, swapped(right)))
-        odds.append(jnp.where(low16, swapped(left), right))
-    squares = jnp.sum(sum(x * x for x in evens + odds), axis=1, keepdims=True)
+
+    squares = jnp.zeros((16, 128), F32)
+    inputs = jnp.zeros((4, 64), F32)
+    gates = jnp.zeros((4, 64), F32)
+    for d in (0, 1, 7, 2, 6, 3, 5, 4):
+        chip = lax.rem(z + d, 8)
+        awaited = [chip * 2 + core, chip * 2 + 1 - core] if d else [b + 1 - 2 * core]
+        for slot in awaited:
+            pltpu.make_async_copy(h2.at[slot], h2.at[slot], chip_sem.at[slot]).wait()
+        left = h2[2 * chip].astype(F32)
+        right = h2[2 * chip + 1].astype(F32)
+        even = jnp.where(low16, left, swapped(right))
+        odd = jnp.where(low16, swapped(left), right)
+        squares = squares + (even * even + odd * odd)
+        block = jnp.concatenate(
+            [
+                (odd if i % 2 else even)[i // 2 * 4 : i // 2 * 4 + 4]
+                * vm["gain"][i * 8 + chip]
+                for i in range(8)
+            ],
+            axis=1,
+        ).astype(BF16)
+
+        def times(weight):
+            part = [
+                weight[:, pl.ds(pl.multiple_of(i * 1024 + chip * 128, 128), 128)]
+                for i in range(8)
+            ]
+            return nt(block, jnp.concatenate(part, axis=1))
+
+        inputs = inputs + times(vm["iw"])
+        gates = gates + times(vm["gw"])
+    squares = jnp.sum(squares, axis=1, keepdims=True)
     square = sum(squares[i * 4 : i * 4 + 4] for i in range(4))
     scale = lax.rsqrt(square * (1.0 / 8192.0) + 1e-5)
-    gain = vm["gain"][...]
-    blocks = []
-    for i in range(64):
-        block = (odds if i // 8 % 2 else evens)[i % 8]
-        row = i // 16 * 4
-        blocks.append(block[row : row + 4] * scale * gain[i : i + 1])
-    normed = jnp.concatenate(blocks, axis=1).astype(BF16)
-    inputs = nt(normed, vm["iw"][...])
+    inputs = inputs * scale
     mixed = silu(conv + inputs * vm["cw"][3:4])
 
     local = jnp.dot(mixed.astype(BF16), vm["pw"][...], preferred_element_type=F32)
@@ -241,7 +263,7 @@
         _, peer = in_yx(d)
         send(p_a, r_pa.at[d - 1], 6, peer)
     pending.append((r_pa, 6))
-    gates = silu(nt(normed, vm["gw"][...]))
+    gates = silu(gates * scale)
     need("sw", "sb", "dl", "sg", "ss", "outw")
     rate = jnp.exp(vm["dl"][...])
     skip = vm["sg"][...] * mixed
@@ -328,7 +350,7 @@
         keys.reshape(4, 512, 128),
         values.reshape(4, 512, 128),
         residual,
-        norm_gain.reshape(64, 128),
+        norm_gain.reshape(64, 1, 128),
         input_weight,
         gate_weight,
         conv_weight,
@@ -352,7 +374,7 @@
         pltpu.VMEM((8, 2, 16, 128), F32),
         pltpu.VMEM((7, 2, 16, 128), F32),
         pltpu.VMEM((16, 16, 128), BF16),
-        pltpu.VMEM((16, 2, 128), F32),
+        pltpu.VMEM((16, 1, 128), F32),
         pltpu.VMEM((4, 4, 128), F32),
         pltpu.VMEM((512, 512), BF16),
         pltpu.VMEM((4, 4, 128), F32),
@@ -370,6 +392,7 @@
         pltpu.VMEM((15, 4, 128), F32),
         pltpu.SemaphoreType.DMA((len(held),)),
         pltpu.SemaphoreType.DMA,
+        pltpu.SemaphoreType.DMA((16,)),
         pltpu.SemaphoreType.DMA((11,)),
         pltpu.SemaphoreType.DMA((11,)),
     ]

time: 56 us -> 53.3 us (0.952)
  Pallas kernels: 54.1 us -> 51.4 us
    pallas_call x1, Pallas kernels: 54.1 us -> 51.4 us  [on_device(): pl.pallas_call(kernel, out_shape=(jax.ShapeDtypeStruct((4, 32), F32), jax...]
where the time goes in v4:
time: 53.3 us; the launch traced here: 53.2 us
  Pallas kernels  51.4 us (96%)
  between operations  0.65 us (1%)
  local copies, waits for them, and re-layouts  0.61 us (1%)
  other arithmetic  0.56 us (1%)
    pallas_call x1, Pallas kernels, on_device(): pl.pallas_call(kernel, out_shape=(jax.ShapeDtypeStruct((4, 32), F32), jax...  51.4 us

profile of v4, /device:TPU:1, one launch (start us, length us, event | category | flops | bytes accessed | tf_op | source)
XLA Modules:
  0.0 53.2 jit_solution(3445597453021317335)
XLA Ops:
  0.6 51.4 %decode_step.1 = (f32[4,32]{1,0:T(4,128)S(1)}, f32[4,16,64]{2,1,0:T(8,128)S(1)}) custom-call(s32[4]{0:T(128)} %refs_0_.1, bf16[4,32,128]{2,1,0:T(8,128)(2,1)} %refs_1_.1, bf16[4,512,128]{2,1,0:T(8,128)(2,1)} %bitcast.7, bf16[4,512,128]{2,1,0:T(8,128)(2,1)} %bitcast.8, bf16[4,64]{1,0:T(4,128)(2,1)} %refs_4_.1, f32[64,1,128]{2,1,0:T(1,128)} %bitcast.9, ...), custom_call_target="tpu_custom_call" | custom-call | tf_op jit(solution)/shard_map/decode_step/pallas_call | solution.py:399
  52.0 0.6 %convert_element_type.3 = bf16[4,32]{1,0:T(4,128)(2,1)} convert(f32[4,32]{1,0:T(4,128)S(1)} %get-tuple-element.4) | non-fusion elementwise | flops 128 | bytes 768 | tf_op jit(solution)/shard_map/convert_element_type | solution.py:416
  52.6 0.6 %copy.22 = f32[4,16,64]{2,1,0:T(8,128)} copy(f32[4,16,64]{2,1,0:T(8,128)S(1)} %get-tuple-element.9) | data formatting | bytes 32768

commit v5 on v4

--- a/solution.py
+++ b/solution.py
@@ -46,7 +46,7 @@
     vm = dict(zip(names_in, refs[n_in + 3 : 2 * n_in + 3]))
     (
         obuf, r_o, ob, mlb, attf, wo, hp, r_hp, h2, p_a, r_pa, rank_b, r_rank,
-        maps_b, r_maps, tb, r_t, tz, r_z, in_sem, own_sem, chip_sem, send_sem, recv_sem,
+        maps_b, r_maps, tb, td, r_d, in_sem, own_sem, chip_sem, send_sem, recv_sem,
     ) = refs[2 * n_in + 3 :]
 
     c = lax.axis_index("ctx")
@@ -78,15 +78,16 @@
         for name in names:
             loads.pop(name).wait()
 
-    first = ("k", "q", "len", "v")
-    for name in first:
-        loads[name].start()
-
     barrier = pltpu.get_barrier_semaphore()
     greeted = [in_b16(d)[1] for d in far_first(16)]
     greeted += [in_a8(d)[1] for d in far_first(8)] + [(c, 1 - h)]
     for peer in greeted:
         pl.semaphore_signal(barrier, 1, device_id=peer, device_id_type=MESH)
+
+    first = ("k", "q", "len", "v")
+    for name in first:
+        loads[name].start()
+
 
     def send(src, dst, stage, peer):
         pltpu.make_async_remote_copy(
@@ -300,40 +301,62 @@
     gated = ((jnp.concatenate(rows, axis=0) + skip) * gates).astype(BF16)
 
     term = jnp.dot(gated, vm["outw"][...], preferred_element_type=F32)
-    for i in range(8):
-        tb[i] = jnp.concatenate(
-            [
-                term[:, (i * 8 + k) * 128 : (i * 8 + k) * 128 + 128]
-                for k in range(8)
-            ],
-            axis=0,
-        ).astype(BF16)
-    for d in far_first(16):
-        other, peer = in_yx(d)
-        send(tb.at[lax.div(other, 2)], r_t.at[d - 1], 9, peer)
-    pending.append((r_t, 9))
+    for i in range(64):
+        tb[i] = term[:, i * 128 : i * 128 + 128]
+    group = lax.div(iota((64, 128), 1), 32)
+    spread = [tb[:, r, :] for r in range(4)]
+    for q in range(4):
+        shares = jnp.zeros((64, 128), F32)
+        for r in range(4):
+            turn = (q - r) % 4 * 32
+            x = spread[r]
+            if turn:
+                x = jnp.concatenate([x[:, turn:], x[:, :turn]], axis=1)
+            shares = jnp.where(group == r, x, shares)
+        td[q] = shares.reshape(64, 1, 128)
+    offsets = [
+        (dy, dx, dz, dc, dh)
+        for dy in range(4)
+        for dx in range(2)
+        for dz in range(8)
+        for dc in range(2)
+        for dh in range(2)
+    ]
+
+    def hops(offset):
+        dy, dx, dz, dc, dh = offset
+        across = (0, 1, 2, 1)[dh * 2 + dx]
+        return min(dy, 4 - dy) + across + min(dz, 8 - dz) + 1.5 * dc
+
+    offsets = sorted(offsets[1:], key=lambda o: -hops(o))
+    y, xl = lax.div(a, 2), lax.rem(a, 2)
+    rows_of = {
+        (dy, dx): lax.rem(y + dy, 4) * 2 + (1 - xl if dx else xl)
+        for dy in range(4)
+        for dx in range(2)
+    }
+    rings = [lax.rem(z + dz, 8) for dz in range(8)]
+    cores = (core, 1 - core)
+    sides = (h, 1 - h)
+    for slot, (dy, dx, dz, dc, dh) in enumerate(offsets):
+        row, ring = rows_of[dy, dx], rings[dz]
+        send(
+            td.at[cores[dc] * 2 + sides[dh], row * 8 + ring], r_d.at[slot], 9,
+            (row * 16 + ring * 2 + cores[dc], sides[dh]),
+        )
+    pending.append((r_d, 9))
     near = h2[b].astype(F32)
     near = sum(
         jnp.where(lax.div(a, 2) == i, near[i * 4 : i * 4 + 4], 0.0) for i in range(4)
     )
-
-    def quarter(block, place):
-        picked = block[:, 0:32]
-        for i in range(1, 4):
-            picked = jnp.where(place == i, block[:, i * 32 : i * 32 + 32], picked)
-        return picked
-
-    own = quarter(near, lax.rem(a, 2) * 2 + h)
-    arrived(r_t, 9)
-    summed = tb[a].astype(F32) + jnp.sum(r_t[...].astype(F32), axis=0)
-    tz[...] = summed.reshape(8, 4, 128)
-    for d in far_first(16):
-        other, peer = in_b16(d)
-        send(tz.at[lax.div(other, 2)], r_z.at[d - 1], 10, peer)
-    pending.append((r_z, 10))
-    arrived(r_z, 10)
-    whole = tz[z] + jnp.sum(r_z[...], axis=0)
-    lo_ref[...] = quarter(whole, core * 2 + h) + own
+    place = lax.rem(a, 2) * 2 + h
+    own = near[:, 0:32]
+    for i in range(1, 4):
+        own = jnp.where(place == i, near[:, i * 32 : i * 32 + 32], own)
+    arrived(r_d, 9)
+    whole = td[core * 2 + h, a * 8 + z] + jnp.sum(r_d[...], axis=0)
+    for r in range(4):
+        lo_ref[r : r + 1] = whole[:, r * 32 : r * 32 + 32] + own[r : r + 1]
 
     for block, stage in pending:
         sent(block, stage)
@@ -386,10 +409,9 @@
         pltpu.VMEM((15, 16, 128), BF16),
         pltpu.VMEM((4, 128), F32),
         pltpu.VMEM((15, 4, 128), F32),
-        pltpu.VMEM((8, 32, 128), BF16),
-        pltpu.VMEM((15, 32, 128), BF16),
-        pltpu.VMEM((8, 4, 128), F32),
-        pltpu.VMEM((15, 4, 128), F32),
+        pltpu.VMEM((64, 4, 128), F32),
+        pltpu.VMEM((4, 64, 1, 128), F32),
+        pltpu.VMEM((255, 1, 128), F32),
         pltpu.SemaphoreType.DMA((len(held),)),
         pltpu.SemaphoreType.DMA,
         pltpu.SemaphoreType.DMA((16,)),

time: 53.3 us -> 50.9 us (0.955)
  Pallas kernels: 51.4 us -> 49 us
    pallas_call x1, Pallas kernels: 51.4 us -> 49 us  [on_device(): pl.pallas_call(kernel, out_shape=(jax.ShapeDtypeStruct((4, 32), F32), jax...]
where the time goes in v5:
time: 50.9 us; the launch traced here: 50.8 us
  Pallas kernels  49 us (96%)
  between operations  0.65 us (1%)
  local copies, waits for them, and re-layouts  0.61 us (1%)
  other arithmetic  0.56 us (1%)
    pallas_call x1, Pallas kernels, on_device(): pl.pallas_call(kernel, out_shape=(jax.ShapeDtypeStruct((4, 32), F32), jax...  49 us

profile of v5, /device:TPU:1, one launch (start us, length us, event | category | flops | bytes accessed | tf_op | source)
XLA Modules:
  0.0 50.8 jit_solution(17123642190979855187)
XLA Ops:
  0.6 49.0 %decode_step.1 = (f32[4,32]{1,0:T(4,128)S(1)}, f32[4,16,64]{2,1,0:T(8,128)S(1)}) custom-call(s32[4]{0:T(128)} %refs_0_.1, bf16[4,32,128]{2,1,0:T(8,128)(2,1)} %refs_1_.1, bf16[4,512,128]{2,1,0:T(8,128)(2,1)} %bitcast.7, bf16[4,512,128]{2,1,0:T(8,128)(2,1)} %bitcast.8, bf16[4,64]{1,0:T(4,128)(2,1)} %refs_4_.1, f32[64,1,128]{2,1,0:T(1,128)} %bitcast.9, ...), custom_call_target="tpu_custom_call" | custom-call | tf_op jit(solution)/shard_map/decode_step/pallas_call | solution.py:421
  49.7 0.6 %convert_element_type.3 = bf16[4,32]{1,0:T(4,128)(2,1)} convert(f32[4,32]{1,0:T(4,128)S(1)} %get-tuple-element.4) | non-fusion elementwise | flops 128 | bytes 768 | tf_op jit(solution)/shard_map/convert_element_type | solution.py:438
  50.2 0.6 %copy.22 = f32[4,16,64]{2,1,0:T(8,128)} copy(f32[4,16,64]{2,1,0:T(8,128)S(1)} %get-tuple-element.9) | data formatting | bytes 32768

commit v6 on v5

--- a/solution.py
+++ b/solution.py
@@ -45,7 +45,7 @@
     lo_ref, ns_ref = refs[n_in + 1 : n_in + 3]
     vm = dict(zip(names_in, refs[n_in + 3 : 2 * n_in + 3]))
     (
-        obuf, r_o, ob, mlb, attf, wo, hp, r_hp, h2, p_a, r_pa, rank_b, r_rank,
+        sums, marks, o0, ml0, r_o, r_ml, ob, mlb, attf, wo, hp, r_hp, h2, p_a, r_pa, rank_b, r_rank,
         maps_b, r_maps, tb, td, r_d, in_sem, own_sem, chip_sem, send_sem, recv_sem,
     ) = refs[2 * n_in + 3 :]
 
@@ -57,17 +57,41 @@
     core = lax.rem(b, 2)
     e = a * 2 + h
 
-    def in_a8(d):
-        other = lax.rem(a + d, 8)
-        return other, (other * 16 + b, h)
-
-    def in_yx(d):
-        other = lax.rem(e + d, 16)
-        return other, (lax.div(other, 2) * 16 + b, lax.rem(other, 2))
-
-    def in_b16(d):
-        other = lax.rem(b + d, 16)
-        return other, (a * 16 + other, h)
+    y, xl = lax.div(a, 2), lax.rem(a, 2)
+    rows_of = {
+        (dy, dx): lax.rem(y + dy, 4) * 2 + (1 - xl if dx else xl)
+        for dy in range(4)
+        for dx in range(2)
+    }
+    rings = [lax.rem(z + dz, 8) for dz in range(8)]
+    cores = (core, 1 - core)
+    sides = (h, 1 - h)
+    offsets = [
+        (dy, dx, dz, dc, dh)
+        for dy in range(4)
+        for dx in range(2)
+        for dz in range(8)
+        for dc in range(2)
+        for dh in range(2)
+    ]
+
+    def hops(offset):
+        dy, dx, dz, dc, dh = offset
+        across = (0, 1, 2, 1)[dh * 2 + dx]
+        return min(dy, 4 - dy) + across + min(dz, 8 - dz) + 1.5 * dc
+
+    offsets = sorted(offsets[1:], key=lambda o: -hops(o))
+
+    def peers(which):
+        found = []
+        for offset in offsets:
+            if all(x == 0 or i in which for i, x in enumerate(offset)):
+                dy, dx, dz, dc, dh = offset
+                row, at = rows_of[dy, dx], rings[dz] * 2 + cores[dc]
+                found.append((row, at, sides[dh], (row * 16 + at, sides[dh])))
+        return found
+
+    a8, yx, b16 = peers((0, 1)), peers((0, 1, 4)), peers((2, 3))
 
     loads = {
         name: pltpu.make_async_copy(hbm[name], vm[name], in_sem.at[i])
@@ -79,8 +103,8 @@
             loads.pop(name).wait()
 
     barrier = pltpu.get_barrier_semaphore()
-    greeted = [in_b16(d)[1] for d in far_first(16)]
-    greeted += [in_a8(d)[1] for d in far_first(8)] + [(c, 1 - h)]
+    greeted = [peer[3] for peer in b16]
+    greeted += [peer[3] for peer in a8] + [(c, 1 - h)]
     for peer in greeted:
         pl.semaphore_signal(barrier, 1, device_id=peer, device_id_type=MESH)
 
@@ -123,22 +147,27 @@
         )
         for i in range(8):
             rows = slice(i * 4, i * 4 + 4)
-            obuf[i, 0, r * 4 : r * 4 + 4] = summed[rows]
-            obuf[i, 1, r * 4 : r * 4 + 4] = jnp.where(low4, high[rows], total[rows])
+            sums[i, r * 4 : r * 4 + 4] = summed[rows]
+            marks[i, r * 4 : r * 4 + 4] = jnp.where(low4, high[rows], total[rows])
+    at = iota((16, 128), 0)
+    on_row = jnp.logical_or(on_diag, lane16 == at + 64)
+    for i in range(8):
+        o0[i] = sums[i].astype(BF16)
+        ml0[i] = jnp.sum(jnp.where(on_row, marks[i], 0.0), axis=0, keepdims=True)
 
     pl.semaphore_wait(barrier, len(greeted))
 
-    for d in far_first(8):
-        other, peer = in_a8(d)
-        send(obuf.at[other], r_o.at[d - 1], 0, peer)
-    sent(r_o, 0)
+    for i, (other, _, _, peer) in enumerate(a8):
+        send(ml0.at[other], r_ml.at[i], 0, peer)
+        send(o0.at[other], r_o.at[i], 11, peer)
+    sent(r_ml.at[pl.ds(0, 7)], 0)
+    sent(r_o.at[pl.ds(0, 7)], 11)
 
     def columns_of(device):
         return ow.at[:, pl.ds(pl.multiple_of(device * 512, 512), 512)]
 
     mine = wo.at[pl.ds(pl.multiple_of(a * 64, 64), 64)]
-    for d in far_first(8):
-        other, peer = in_a8(d)
+    for other, _, _, peer in a8:
         send(columns_of(other), mine, 1, peer)
     pending.append((wo.at[pl.ds(0, 448)], 1))
     own_columns = pltpu.make_async_copy(columns_of(a), mine, own_sem)
@@ -147,43 +176,41 @@
         if name not in first:
             loads[name].start()
 
-    arrived(r_o, 0)
-    low16 = lane16 < 64
-
     def swapped(x):
         return jnp.concatenate([x[:, 64:], x[:, :64]], axis=1)
 
-    outs = [obuf[a, 0]] + [r_o[i, 0] for i in range(7)]
-    marks = [obuf[a, 1]] + [r_o[i, 1] for i in range(7)]
-    highs = [jnp.where(low16, x, swapped(x)) for x in marks]
-    top = functools.reduce(jnp.maximum, highs)
-    scales = [jnp.exp(x - top) for x in highs]
-    total = sum(s * x for s, x in zip(scales, marks))
-    summed = sum(s * x for s, x in zip(scales, outs))
+    low1 = iota((1, 128), 1) < 64
+    filled = iota((1, 128), 1) < 16
+
+    def weigh(marks):
+        top = jnp.max(marks, axis=0, keepdims=True)
+        scales = jnp.exp(marks - top)
+        return scales, top, jnp.sum(scales * swapped(marks), axis=0, keepdims=True)
+
+    def column(row):
+        return jnp.sum(jnp.where(on_diag, row, 0.0), axis=1, keepdims=True)
+
+    arrived(r_ml.at[pl.ds(0, 7)], 0)
+    r_ml[7] = ml0[a]
+    scales, top, total = weigh(r_ml[:, 0, :])
+    scales = [column(scales[i : i + 1]) for i in range(8)]
+    arrived(r_o.at[pl.ds(0, 7)], 11)
+    r_o[7] = o0[a]
+    summed = sum(scales[i] * r_o[i].astype(F32) for i in range(8))
 
     ob[b] = summed.astype(BF16)
-    packed = jnp.where(low16, top, total)
-    both = jnp.logical_or(on_diag, lane16 == iota((16, 128), 0) + 64)
-    mlb[b] = jnp.sum(jnp.where(both, packed, 0.0), axis=0, keepdims=True)
-    for d in far_first(16):
-        _, peer = in_b16(d)
+    mlb[b] = jnp.where(low1, top, swapped(total))
+    for _, _, _, peer in b16:
         send(mlb.at[b], mlb.at[b], 2, peer)
         send(ob.at[b], ob.at[b], 3, peer)
     pending.append((mlb.at[pl.ds(0, 15)], 2))
     pending.append((ob.at[pl.ds(0, 15)], 3))
     arrived(mlb.at[pl.ds(0, 15)], 2)
-    high_rows = mlb[:, 0, :]
-    total_rows = swapped(high_rows)
-    scale_rows = jnp.exp(high_rows - jnp.max(high_rows, axis=0, keepdims=True))
-    all_total = jnp.sum(scale_rows * total_rows, axis=0, keepdims=True)
-    valid = iota((1, 128), 1) < 16
-    scale_rows = scale_rows / jnp.where(valid, all_total, 1.0)
-    columns = [
-        jnp.sum(jnp.where(on_diag, scale_rows[i : i + 1], 0.0), axis=1, keepdims=True)
-        for i in range(16)
-    ]
+    scales, _, total = weigh(mlb[:, 0, :])
+    scales = scales / jnp.where(filled, total, 1.0)
+    scales = [column(scales[i : i + 1]) for i in range(16)]
     arrived(ob.at[pl.ds(0, 15)], 3)
-    attended = sum(columns[i] * ob[i].astype(F32) for i in range(16))
+    attended = sum(scales[i] * ob[i].astype(F32) for i in range(16))
 
     for r in range(4):
         attf[r] = attended[r * 4 : r * 4 + 4]
@@ -201,14 +228,12 @@
             lax.div(a, 2) == i, rest, 0.0
         )
 
-    for d in far_first(16):
-        _, peer = in_yx(d)
-        send(hp, r_hp.at[d - 1], 4, peer)
+    for i, (_, _, _, peer) in enumerate(yx):
+        send(hp, r_hp.at[i], 4, peer)
     pending.append((r_hp, 4))
     arrived(r_hp, 4)
     h2[b] = (hp[...] + jnp.sum(r_hp[...], axis=0)).reshape(16, 128).astype(BF16)
-    for d in far_first(16):
-        _, peer = in_b16(d)
+    for _, _, _, peer in b16:
         pltpu.make_async_remote_copy(
             h2.at[b], h2.at[b], send_sem.at[5], chip_sem.at[b],
             device_id=peer, device_id_type=MESH,
@@ -219,6 +244,7 @@
     for i in range(3):
         conv = conv + vm["cs"][i].astype(F32) * vm["cw"][i : i + 1]
 
+    low16 = lane16 < 64
     squares = jnp.zeros((16, 128), F32)
     inputs = jnp.zeros((4, 64), F32)
     gates = jnp.zeros((4, 64), F32)
@@ -260,9 +286,8 @@
     for i in range(4):
         p_a[i] = local[:, i * 128 : i * 128 + 128]
     p_a[4] = jnp.concatenate([local[:, 512:544], jnp.zeros((4, 96), F32)], axis=1)
-    for d in far_first(16):
-        _, peer = in_yx(d)
-        send(p_a, r_pa.at[d - 1], 6, peer)
+    for i, (_, _, _, peer) in enumerate(yx):
+        send(p_a, r_pa.at[i], 6, peer)
     pending.append((r_pa, 6))
     gates = silu(gates * scale)
     need("sw", "sb", "dl", "sg", "ss", "outw")
@@ -273,10 +298,9 @@
     ranks = projected[0:4].reshape(16, 128)
     rank_b[...] = ranks.astype(BF16)
     maps_b[...] = projected[4]
-    for d in far_first(16):
-        _, peer = in_b16(d)
-        send(rank_b, r_rank.at[d - 1], 7, peer)
-        send(maps_b, r_maps.at[d - 1], 8, peer)
+    for i, (_, _, _, peer) in enumerate(b16):
+        send(rank_b, r_rank.at[i], 7, peer)
+        send(maps_b, r_maps.at[i], 8, peer)
     pending.append((r_rank, 7))
     pending.append((r_maps, 8))
     arrived(r_rank, 7)
@@ -314,36 +338,9 @@
                 x = jnp.concatenate([x[:, turn:], x[:, :turn]], axis=1)
             shares = jnp.where(group == r, x, shares)
         td[q] = shares.reshape(64, 1, 128)
-    offsets = [
-        (dy, dx, dz, dc, dh)
-        for dy in range(4)
-        for dx in range(2)
-        for dz in range(8)
-        for dc in range(2)
-        for dh in range(2)
-    ]
-
-    def hops(offset):
-        dy, dx, dz, dc, dh = offset
-        across = (0, 1, 2, 1)[dh * 2 + dx]
-        return min(dy, 4 - dy) + across + min(dz, 8 - dz) + 1.5 * dc
-
-    offsets = sorted(offsets[1:], key=lambda o: -hops(o))
-    y, xl = lax.div(a, 2), lax.rem(a, 2)
-    rows_of = {
-        (dy, dx): lax.rem(y + dy, 4) * 2 + (1 - xl if dx else xl)
-        for dy in range(4)
-        for dx in range(2)
-    }
-    rings = [lax.rem(z + dz, 8) for dz in range(8)]
-    cores = (core, 1 - core)
-    sides = (h, 1 - h)
-    for slot, (dy, dx, dz, dc, dh) in enumerate(offsets):
-        row, ring = rows_of[dy, dx], rings[dz]
-        send(
-            td.at[cores[dc] * 2 + sides[dh], row * 8 + ring], r_d.at[slot], 9,
-            (row * 16 + ring * 2 + cores[dc], sides[dh]),
-        )
+    for i, (row, at, side, peer) in enumerate(peers((0, 1, 2, 3, 4))):
+        share = td.at[lax.rem(at, 2) * 2 + side, row * 8 + lax.div(at, 2)]
+        send(share, r_d.at[i], 9, peer)
     pending.append((r_d, 9))
     near = h2[b].astype(F32)
     near = sum(
@@ -355,8 +352,8 @@
         own = jnp.where(place == i, near[:, i * 32 : i * 32 + 32], own)
     arrived(r_d, 9)
     whole = td[core * 2 + h, a * 8 + z] + jnp.sum(r_d[...], axis=0)
-    for r in range(4):
-        lo_ref[r : r + 1] = whole[:, r * 32 : r * 32 + 32] + own[r : r + 1]
+    shares = [whole[:, r * 32 : r * 32 + 32] for r in range(4)]
+    lo_ref[...] = (jnp.concatenate(shares, axis=0) + own).astype(BF16)
 
     for block, stage in pending:
         sent(block, stage)
@@ -394,8 +391,12 @@
         for x in operands + (out_weight,)
     ]
     scratch = [
-        pltpu.VMEM((8, 2, 16, 128), F32),
-        pltpu.VMEM((7, 2, 16, 128), F32),
+        pltpu.VMEM((8, 16, 128), F32),
+        pltpu.VMEM((8, 16, 128), F32),
+        pltpu.VMEM((8, 16, 128), BF16),
+        pltpu.VMEM((8, 1, 128), F32),
+        pltpu.VMEM((8, 16, 128), BF16),
+        pltpu.VMEM((8, 1, 128), F32),
         pltpu.VMEM((16, 16, 128), BF16),
         pltpu.VMEM((16, 1, 128), F32),
         pltpu.VMEM((4, 4, 128), F32),
@@ -415,13 +416,13 @@
         pltpu.SemaphoreType.DMA((len(held),)),
         pltpu.SemaphoreType.DMA,
         pltpu.SemaphoreType.DMA((16,)),
-        pltpu.SemaphoreType.DMA((11,)),
-        pltpu.SemaphoreType.DMA((11,)),
+        pltpu.SemaphoreType.DMA((12,)),
+        pltpu.SemaphoreType.DMA((12,)),
     ]
     layer_out, new_state = pl.pallas_call(
         kernel,
         out_shape=(
-            jax.ShapeDtypeStruct((4, 32), F32),
+            jax.ShapeDtypeStruct((4, 32), BF16),
             jax.ShapeDtypeStruct((4, 16, 64), F32),
         ),
         in_specs=[pl.BlockSpec(memory_space=pltpu.HBM)] * len(operands),
@@ -435,7 +436,7 @@
         ),
         name="decode_step",
     )(*operands)
-    return layer_out.astype(BF16), new_state
+    return layer_out, new_state
 
 
 def solution(mesh):

time: 50.9 us -> 49.9 us (0.980)
  Pallas kernels: 49 us -> 48 us
  local copies, waits for them, and re-layouts: 0.61 us -> 1.18 us
  other arithmetic: 0.56 us -> 0 us
    pallas_call x1, Pallas kernels: 49 us -> 48 us  [on_device(): pl.pallas_call(kernel, out_shape=(jax.ShapeDtypeStruct((4, 32), BF16), ja...]
    unnamed x1 -> x2, local copies, waits for them, and re-layouts: 0.61 us -> 1.18 us
    convert_element_type x1 -> x0, other arithmetic: 0.56 us -> none  [on_device(): return (layer_out.astype(BF16), new_state)]
where the time goes in v6:
time: 49.9 us; the launch traced here: 49.8 us
  Pallas kernels  48 us (96%)
  local copies, waits for them, and re-layouts  1.18 us (2%)
  between operations  0.65 us (1%)
    pallas_call x1, Pallas kernels, on_device(): pl.pallas_call(kernel, out_shape=(jax.ShapeDtypeStruct((4, 32), BF16), ja...  48 us
    unnamed x2, local copies, waits for them, and re-layouts  1.18 us

profile of v6, /device:TPU:1, one launch (start us, length us, event | category | flops | bytes accessed | tf_op | source)
XLA Modules:
  0.0 49.8 jit_solution(12971701490694011332)
XLA Ops:
  0.6 48.0 %decode_step.1 = (bf16[4,32]{1,0:T(4,128)(2,1)S(1)}, f32[4,16,64]{2,1,0:T(8,128)S(1)}) custom-call(s32[4]{0:T(128)} %refs_0_.1, bf16[4,32,128]{2,1,0:T(8,128)(2,1)} %refs_1_.1, bf16[4,512,128]{2,1,0:T(8,128)(2,1)} %bitcast.7, bf16[4,512,128]{2,1,0:T(8,128)(2,1)} %bitcast.8, bf16[4,64]{1,0:T(4,128)(2,1)} %refs_4_.1, f32[64,1,128]{2,1,0:T(1,128)} %bitcast.9, ...), custom_call_target="tpu_custom_call" | custom-call | tf_op jit(solution)/shard_map/decode_step/pallas_call | solution.py:422
  48.6 0.6 %copy.23 = bf16[4,32]{1,0:T(4,128)(2,1)} copy(bf16[4,32]{1,0:T(4,128)(2,1)S(1)} %get-tuple-element.4) | data formatting | bytes 512
  49.2 0.6 %copy.24 = f32[4,16,64]{2,1,0:T(8,128)} copy(f32[4,16,64]{2,1,0:T(8,128)S(1)} %get-tuple-element.5) | data formatting | bytes 32768

commit v7 on v6

--- a/solution.py
+++ b/solution.py
@@ -167,9 +167,8 @@
         return ow.at[:, pl.ds(pl.multiple_of(device * 512, 512), 512)]
 
     mine = wo.at[pl.ds(pl.multiple_of(a * 64, 64), 64)]
-    for other, _, _, peer in a8:
+    for other, _, _, peer in a8[:4]:
         send(columns_of(other), mine, 1, peer)
-    pending.append((wo.at[pl.ds(0, 448)], 1))
     own_columns = pltpu.make_async_copy(columns_of(a), mine, own_sem)
     own_columns.start()
     for name in names_in:
@@ -191,6 +190,9 @@
         return jnp.sum(jnp.where(on_diag, row, 0.0), axis=1, keepdims=True)
 
     arrived(r_ml.at[pl.ds(0, 7)], 0)
+    for other, _, _, peer in a8[4:]:
+        send(columns_of(other), mine, 1, peer)
+    pending.append((wo.at[pl.ds(0, 448)], 1))
     r_ml[7] = ml0[a]
     scales, top, total = weigh(r_ml[:, 0, :])
     scales = [column(scales[i : i + 1]) for i in range(8)]

time: 49.9 us -> 49.7 us (level)
  no operation moved by 1% of the time
where the time goes in v7:
time: 49.7 us; the launch traced here: 49.6 us
  Pallas kernels  47.7 us (96%)
  local copies, waits for them, and re-layouts  1.18 us (2%)
  between operations  0.65 us (1%)
    pallas_call x1, Pallas kernels, on_device(): pl.pallas_call(kernel, out_shape=(jax.ShapeDtypeStruct((4, 32), BF16), ja...  47.7 us
    unnamed x2, local copies, waits for them, and re-layouts  1.18 us

profile of v7, /device:TPU:1, one launch (start us, length us, event | category | flops | bytes accessed | tf_op | source)
XLA Modules:
  0.0 49.6 jit_solution(4998906167545488574)
XLA Ops:
  0.6 47.7 %decode_step.1 = (bf16[4,32]{1,0:T(4,128)(2,1)S(1)}, f32[4,16,64]{2,1,0:T(8,128)S(1)}) custom-call(s32[4]{0:T(128)} %refs_0_.1, bf16[4,32,128]{2,1,0:T(8,128)(2,1)} %refs_1_.1, bf16[4,512,128]{2,1,0:T(8,128)(2,1)} %bitcast.7, bf16[4,512,128]{2,1,0:T(8,128)(2,1)} %bitcast.8, bf16[4,64]{1,0:T(4,128)(2,1)} %refs_4_.1, f32[64,1,128]{2,1,0:T(1,128)} %bitcast.9, ...), custom_call_target="tpu_custom_call" | custom-call | tf_op jit(solution)/shard_map/decode_step/pallas_call | solution.py:424
  48.4 0.6 %copy.23 = bf16[4,32]{1,0:T(4,128)(2,1)} copy(bf16[4,32]{1,0:T(4,128)(2,1)S(1)} %get-tuple-element.4) | data formatting | bytes 512
  48.9 0.6 %copy.24 = f32[4,16,64]{2,1,0:T(8,128)} copy(f32[4,16,64]{2,1,0:T(8,128)S(1)} %get-tuple-element.5) | data formatting | bytes 32768

commit v8 on v7

--- a/solution.py
+++ b/solution.py
@@ -225,16 +225,21 @@
     twice = jnp.concatenate([rest, rest], axis=1)
     adds = jnp.logical_and(low4 == (lax.rem(a, 2) == 0), h == 0)
     rest = jnp.where(adds, twice, 0.0)
-    for i in range(4):
-        hp[i] = partial[:, i * 128 : i * 128 + 128] + jnp.where(
-            lax.div(a, 2) == i, rest, 0.0
-        )
+    partial = jnp.concatenate(
+        [
+            partial[:, i * 128 : i * 128 + 128]
+            + jnp.where(lax.div(a, 2) == i, rest, 0.0)
+            for i in range(4)
+        ],
+        axis=0,
+    )
+    hp[...] = partial.astype(BF16)
 
     for i, (_, _, _, peer) in enumerate(yx):
         send(hp, r_hp.at[i], 4, peer)
     pending.append((r_hp, 4))
     arrived(r_hp, 4)
-    h2[b] = (hp[...] + jnp.sum(r_hp[...], axis=0)).reshape(16, 128).astype(BF16)
+    h2[b] = (partial + jnp.sum(r_hp[...].astype(F32), axis=0)).astype(BF16)
     for _, _, _, peer in b16:
         pltpu.make_async_remote_copy(
             h2.at[b], h2.at[b], send_sem.at[5], chip_sem.at[b],
@@ -299,7 +304,9 @@
     projected = p_a[...] + jnp.sum(r_pa[...], axis=0)
     ranks = projected[0:4].reshape(16, 128)
     rank_b[...] = ranks.astype(BF16)
-    maps_b[...] = projected[4]
+    maps_b[...] = jnp.concatenate(
+        [projected[4, r : r + 1, 0:32] for r in range(4)], axis=1
+    )
     for i, (_, _, _, peer) in enumerate(b16):
         send(rank_b, r_rank.at[i], 7, peer)
         send(maps_b, r_maps.at[i], 8, peer)
@@ -314,12 +321,13 @@
         [ranks[i * 4 : i * 4 + 4] for i in range(4)], axis=1
     ).astype(BF16)
     step = softplus(nt(rank, vm["sw"][...]) + vm["sb"][...])
-    pick_leave = lane16 == iota((16, 128), 0) + 16
+    state_row = iota((16, 128), 0)
     rows = []
     for r in range(4):
-        row = maps[r : r + 1]
-        entry = jnp.sum(jnp.where(on_diag, row, 0.0), axis=1, keepdims=True)
-        leave = jnp.sum(jnp.where(pick_leave, row, 0.0), axis=1, keepdims=True)
+        pick = lane16 == state_row + r * 32
+        entry = jnp.sum(jnp.where(pick, maps, 0.0), axis=1, keepdims=True)
+        pick = lane16 == state_row + r * 32 + 16
+        leave = jnp.sum(jnp.where(pick, maps, 0.0), axis=1, keepdims=True)
         step_r = step[r : r + 1]
         state = jnp.exp(-step_r * rate) * vm["ss"][r] + entry * (step_r * mixed[r : r + 1])
         ns_ref[r] = state
@@ -403,15 +411,15 @@
         pltpu.VMEM((16, 1, 128), F32),
         pltpu.VMEM((4, 4, 128), F32),
         pltpu.VMEM((512, 512), BF16),
-        pltpu.VMEM((4, 4, 128), F32),
-        pltpu.VMEM((15, 4, 4, 128), F32),
+        pltpu.VMEM((16, 128), BF16),
+        pltpu.VMEM((15, 16, 128), BF16),
         pltpu.VMEM((16, 16, 128), BF16),
         pltpu.VMEM((5, 4, 128), F32),
         pltpu.VMEM((15, 5, 4, 128), F32),
         pltpu.VMEM((16, 128), BF16),
         pltpu.VMEM((15, 16, 128), BF16),
-        pltpu.VMEM((4, 128), F32),
-        pltpu.VMEM((15, 4, 128), F32),
+        pltpu.VMEM((1, 128), F32),
+        pltpu.VMEM((15, 1, 128), F32),
         pltpu.VMEM((64, 4, 128), F32),
         pltpu.VMEM((4, 64, 1, 128), F32),
         pltpu.VMEM((255, 1, 128), F32),

time: 49.7 us -> 49.7 us (level)
  no operation moved by 1% of the time
where the time goes in v8:
time: 49.7 us; the launch traced here: 49.6 us
  Pallas kernels  47.8 us (96%)
  local copies, waits for them, and re-layouts  1.18 us (2%)
  between operations  0.65 us (1%)
    pallas_call x1, Pallas kernels, on_device(): pl.pallas_call(kernel, out_shape=(jax.ShapeDtypeStruct((4, 32), BF16), ja...  47.8 us
    unnamed x2, local copies, waits for them, and re-layouts  1.18 us

profile of v8, /device:TPU:1, one launch (start us, length us, event | category | flops | bytes accessed | tf_op | source)
XLA Modules:
  0.0 49.6 jit_solution(17296385163977962664)
XLA Ops:
  0.6 47.8 %decode_step.1 = (bf16[4,32]{1,0:T(4,128)(2,1)S(1)}, f32[4,16,64]{2,1,0:T(8,128)S(1)}) custom-call(s32[4]{0:T(128)} %refs_0_.1, bf16[4,32,128]{2,1,0:T(8,128)(2,1)} %refs_1_.1, bf16[4,512,128]{2,1,0:T(8,128)(2,1)} %bitcast.7, bf16[4,512,128]{2,1,0:T(8,128)(2,1)} %bitcast.8, bf16[4,64]{1,0:T(4,128)(2,1)} %refs_4_.1, f32[64,1,128]{2,1,0:T(1,128)} %bitcast.9, ...), custom_call_target="tpu_custom_call" | custom-call | tf_op jit(solution)/shard_map/decode_step/pallas_call | solution.py:432
  48.5 0.6 %copy.23 = bf16[4,32]{1,0:T(4,128)(2,1)} copy(bf16[4,32]{1,0:T(4,128)(2,1)S(1)} %get-tuple-element.4) | data formatting | bytes 512
  49.0 0.6 %copy.24 = f32[4,16,64]{2,1,0:T(8,128)} copy(f32[4,16,64]{2,1,0:T(8,128)S(1)} %get-tuple-element.5) | data formatting | bytes 32768
